TPU v7x, 128 devices: a whole 4x4x4 slice. The times are simulated.
128 devices in a mesh: ch: 32 (over x, y, z_hi), half: 4 (over z_lo, core).
Axes of the slice: x: 4, y: 4, z: 4 (z_hi: 2, z_lo: 2; z = z_hi * 2 + z_lo), core: 2. Of those that a mesh axis runs over, the one named last changes fastest.
Arguments:
- pair_act: bfloat16 [768, 768, 128], P('half', 'ch'), may hold values from -6 to 6
- tri_out: bfloat16 [768, 768, 128], P('half', 'ch'), may hold values from -48 to 48
- cotangent: bfloat16 [768, 768, 128], P('half', 'ch'), may hold values from -6 to 6
- residue_mask: int32 [768], replicated, may hold values 0 or 1
- chain_index: int32 [768], replicated, may hold values from 0 to 3, never falling along the last dimension, each value on 1 to 384 neighbouring positions
- chain_pairs: int32 [4, 4], replicated, may hold values 0 or 1
- in_weight: bfloat16 [128, 640], replicated, may hold values from -0.5 to 0.5
- out_weight: bfloat16 [128, 128], replicated, may hold values from -0.5 to 0.5
- in_gain: float32 [128], replicated, may hold values from 0.1 to 1.9
- in_bias: float32 [128], replicated, may hold values from -3 to 3
- out_gain: float32 [128], replicated, may hold values from 0.1 to 1.9
- out_bias: float32 [128], replicated, may hold values from -3 to 3
Outputs:
- grad_pair: bfloat16 [768, 768, 128], P('half', 'ch')
Inputs may be any that keep to these rules, and one draw needn't show every extreme that they name: `chain_index`: chains are numbered in order along the residues, never falling; one chain has 384 residues.
All inputs are finite; a program needn't handle non-finite values.
Results may differ from a plain program's by a relative error of at most 0.015.
Values may be sent and summed in bfloat16 or wider, within the bound.
No kernel may reach another device: no remote copies, remote signals or barrier semaphores. Data moves between devices by JAX's collectives and lax.ppermute only.
A program may use at most 128 MiB of HBM per device.

v0:
```python
import jax
import jax.numpy as jnp
from jax import lax
from jax.sharding import PartitionSpec as P

EPSILON = 1e-05


def normalize(values, gain, bias):
    centre = jnp.mean(values, -1, keepdims=True)
    centred = values - centre
    inv_scale = lax.rsqrt(jnp.mean(centred * centred, -1, keepdims=True) + EPSILON)
    unit_val = centred * inv_scale
    return (unit_val * gain + bias, unit_val, inv_scale)


def norm_back(grad_in, unit_val, inv_scale):
    first_mean = jnp.mean(grad_in, -1, keepdims=True)
    second_mean = jnp.mean(grad_in * unit_val, -1, keepdims=True)
    return inv_scale * (grad_in - first_mean - unit_val * second_mean)


def tile_keep(residue_mask, chain_index, chain_pairs, row_start, row_count, col_start, col_count):
    labels = jnp.arange(chain_pairs.shape[0], dtype=jnp.int32)
    row_chain = lax.dynamic_slice_in_dim(chain_index, row_start, row_count)
    col_chain = lax.dynamic_slice_in_dim(chain_index, col_start, col_count)
    row_onehot = (row_chain[:, None] == labels[None, :]).astype(jnp.float32)
    col_onehot = (col_chain[:, None] == labels[None, :]).astype(jnp.float32)
    allowed = jnp.dot(jnp.dot(row_onehot, chain_pairs.astype(jnp.float32)), col_onehot.T)
    row_res = lax.dynamic_slice_in_dim(residue_mask, row_start, row_count).astype(jnp.float32)
    col_res = lax.dynamic_slice_in_dim(residue_mask, col_start, col_count).astype(jnp.float32)
    return allowed * row_res[:, None] * col_res[None, :]


def on_device(
    pair_act,
    tri_out,
    cotangent,
    residue_mask,
    chain_index,
    chain_pairs,
    in_weight,
    out_weight,
    in_gain,
    in_bias,
    out_gain,
    out_bias,
):
    row_count, col_count, channels = pair_act.shape
    keep = tile_keep(
        residue_mask,
        chain_index,
        chain_pairs,
        lax.axis_index("half") * row_count,
        row_count,
        lax.axis_index("ch") * col_count,
        col_count,
    )
    keep_col = keep[:, :, None]
    normed, unit_z, inv_z = normalize(pair_act.astype(jnp.float32), in_gain, in_bias)
    projected = jnp.einsum(
        "ikd,de->ike", normed.astype(jnp.bfloat16), in_weight, preferred_element_type=jnp.float32
    )
    left_proj = projected[..., :channels]
    left_gate = jax.nn.sigmoid(projected[..., channels : 2 * channels])
    right_proj = projected[..., 2 * channels : 3 * channels]
    right_gate = jax.nn.sigmoid(projected[..., 3 * channels : 4 * channels])
    out_gate = jax.nn.sigmoid(projected[..., 4 * channels :])
    left = (keep_col * left_gate * left_proj).astype(jnp.bfloat16)
    right = (keep_col * right_gate * right_proj).astype(jnp.bfloat16)
    normed_x, unit_x, inv_x = normalize(tri_out.astype(jnp.float32), out_gain, out_bias)
    out_proj = jnp.einsum(
        "ikc,cd->ikd", normed_x.astype(jnp.bfloat16), out_weight, preferred_element_type=jnp.float32
    )
    grad_gate = cotangent * out_proj
    grad_outer = (cotangent * out_gate).astype(jnp.bfloat16)
    grad_normed = jnp.einsum(
        "ikd,cd->ikc", grad_outer, out_weight, preferred_element_type=jnp.float32
    )
    grad_tri = norm_back(grad_normed * out_gain, unit_x, inv_x).astype(jnp.bfloat16)
    outgoing = (
        jnp.transpose(grad_tri, (0, 2, 1)),
        jnp.transpose(left, (0, 2, 1)),
        jnp.transpose(right, (0, 2, 1)),
    )
    grad_ch, left_ch, right_ch = (
        lax.all_to_all(outgoing[0], "ch", split_axis=1, concat_axis=2, tiled=True),
        lax.all_to_all(outgoing[1], "ch", split_axis=1, concat_axis=2, tiled=True),
        lax.all_to_all(outgoing[2], "ch", split_axis=1, concat_axis=2, tiled=True),
    )
    grad_block = grad_ch
    grad_left = jnp.einsum(
        "icj,jck->ick",
        grad_block,
        lax.all_gather(right_ch, "half", axis=0, tiled=True),
        preferred_element_type=jnp.float32,
    )
    grad_block = grad_ch
    grad_right = lax.psum_scatter(
        jnp.einsum("icj,ick->jck", grad_block, left_ch, preferred_element_type=jnp.float32).astype(
            jnp.bfloat16
        ),
        "half",
        scatter_dimension=0,
        tiled=True,
    )
    back_left, back_right = (
        lax.all_to_all(
            grad_left.astype(jnp.bfloat16), "ch", split_axis=2, concat_axis=1, tiled=True
        ),
        lax.all_to_all(grad_right, "ch", split_axis=2, concat_axis=1, tiled=True),
    )
    tile_left = jnp.transpose(back_left, (0, 2, 1))
    tile_right = jnp.transpose(back_right, (0, 2, 1))
    grad_l = tile_left.astype(jnp.float32) * keep_col
    grad_r = tile_right.astype(jnp.float32) * keep_col
    grad_proj = jnp.concatenate(
        [
            grad_l * left_gate,
            grad_l * left_proj * left_gate * (1.0 - left_gate),
            grad_r * right_gate,
            grad_r * right_proj * right_gate * (1.0 - right_gate),
            grad_gate * out_gate * (1.0 - out_gate),
        ],
        -1,
    ).astype(jnp.bfloat16)
    grad_normed_z = jnp.einsum(
        "ike,de->ikd", grad_proj, in_weight, preferred_element_type=jnp.float32
    )
    return norm_back(grad_normed_z * in_gain, unit_z, inv_z).astype(jnp.bfloat16)


def solution(mesh):
    return jax.shard_map(
        on_device,
        mesh=mesh,
        in_specs=(
            P("half", "ch", None),
            P("half", "ch", None),
            P("half", "ch", None),
            P(),
            P(),
            P(),
            P(),
            P(),
            P(),
            P(),
            P(),
            P(),
        ),
        out_specs=P("half", "ch", None),
        check_vma=False,
    )
```

profile of v0, /device:TPU:1, one launch (start us, length us, event | category | flops | bytes accessed | tf_op | source)
XLA Modules:
  0.0 363.9 jit_solution(13603671513677908665)
XLA Ops:
  17.7 3.5 fusion.48
  24.9 11.3 %all-to-all-start.3 = ((bf16[192,128,24]{0,2,1:T(8,128)(2,1)}), bf16[192,128,24]{0,2,1:T(8,128)(2,1)S(1)}, u32[]{:S(2)}, u32[]{:S(2)}) async-start(bf16[192,128,24]{0,2,1:T(8,128)(2,1)} %copy.72), calls=%async_computation.3 | async-start | bytes 3145728 | tf_op jit(solution)/shard_map/all_to_all | solution.py:88
  38.4 4.5 %multiply_reduce_fusion.1 = (f32[192,24]{1,0:T(8,128)S(1)}, f32[192,24]{1,0:T(8,128)S(1)}, f32[192,24,128]{2,1,0:T(8,128)S(1)}) fusion(f32[128]{0:T(128)S(1)} %copy-done.16, f32[192,24]{1,0:T(8,128)S(1)} %add_rsqrt_fusion, f32[192,24]{1,0:T(8,128)S(1)} %broadcast_multiply_fusion.4, bf16[192,24,128]{2,1,0:T(8,128)(2,1)S(1)} %copy-done.5, ...), kind=kOutput, calls=%fused_computation.63 | convolution fusion | flops 158653440 | bytes 7184896 | tf_op jit(solution)/shard_map/ikd,cd->ikc/dot_general | solution.py:77
  42.9 4.0 %fusion.58 = bf16[192,128,24]{1,2,0:T(8,128)(2,1)} fusion(bf16[192,24,128]{2,1,0:T(8,128)(2,1)S(1)} %copy-done.5, f32[192,24,128]{2,1,0:T(8,128)S(1)} %get-tuple-element.11, f32[192,24]{1,0:T(8,128)S(1)} %get-tuple-element.13, f32[192,24]{1,0:T(8,128)S(1)} %get-tuple-element.14, f32[128]{0:T(128)S(1)} %copy-done.16, f32[192,24]{1,0:T(8,128)S(1)} %add_rsqrt_fusion, ...), kind=kLoop, calls=%fused_computation.75 | loop fusion | flops 5308416 | bytes 4792832 | tf_op jit(solution)/shard_map/transpose | solution.py:82
  46.9 3.3 copy.64
  50.3 9.1 %all-to-all-done.3 = bf16[192,128,24]{0,2,1:T(8,128)(2,1)S(1)} async-done(((bf16[192,128,24]{0,2,1:T(8,128)(2,1)}), bf16[192,128,24]{0,2,1:T(8,128)(2,1)S(1)}, u32[]{:S(2)}, u32[]{:S(2)}) %all-to-all-start.3) | async-done | bytes 1179680 | tf_op jit(solution)/shard_map/all_to_all | solution.py:88
  59.3 4.7 %all-to-all-start.1 = ((bf16[192,128,24]{0,2,1:T(8,128)(2,1)}), bf16[192,128,24]{0,2,1:T(8,128)(2,1)}, u32[]{:S(2)}, u32[]{:S(2)}) async-start(bf16[192,128,24]{0,2,1:T(8,128)(2,1)} %copy.64), calls=%async_computation.1 | async-start | bytes 3145728 | tf_op jit(solution)/shard_map/all_to_all | solution.py:87
  65.4 20.1 %all-to-all-done.1 = bf16[192,128,24]{0,2,1:T(8,128)(2,1)} async-done(((bf16[192,128,24]{0,2,1:T(8,128)(2,1)}), bf16[192,128,24]{0,2,1:T(8,128)(2,1)}, u32[]{:S(2)}, u32[]{:S(2)}) %all-to-all-start.1) | async-done | bytes 1179680 | tf_op jit(solution)/shard_map/all_to_all | solution.py:87
  87.0 3.6 convert_bitcast_fusion
  90.5 8.5 %copy.76 = bf16[768,4,768]{2,1,0:T(4,128)(2,1)} copy(bf16[768,4,768]{0,2,1:T(8,128)(2,1)} %convert_bitcast_fusion) | data formatting | bytes 9437184 | tf_op jit(solution)/shard_map/convert_element_type | solution.py:100
  102.0 28.1 %all_to_all.72 = bf16[192,128,24]{0,2,1:T(8,128)(2,1)S(1)} all-to-all(bf16[192,128,24]{0,2,1:T(8,128)(2,1)S(1)} %copy.61), channel_id=1, replica_groups=mesh['ch'=32,'half'=4] {'ch'}, dimensions={1} | all-to-all | bytes 2359296 | tf_op jit(solution)/shard_map/all_to_all | solution.py:89
  133.0 82.9 %all-reduce.3.cloned.1.call-done = bf16[768,4,768]{2,1,0:T(4,128)(2,1)} async-done(((bf16[768,4,768]{2,1,0:T(4,128)(2,1)}), bf16[768,4,768]{2,1,0:T(4,128)(2,1)}) %all-reduce.3.cloned.1.call-update) | async-done | bytes 4718608
  220.1 9.1 %all-to-all-start.4 = ((bf16[192,4,768]{0,1,2:T(4,128)(2,1)}), bf16[192,4,768]{0,1,2:T(4,128)(2,1)S(1)}, u32[]{:S(2)}, u32[]{:S(2)}) async-start(bf16[192,4,768]{0,1,2:T(4,128)(2,1)} %copy.77), calls=%async_computation.4 | async-start | bytes 3145728 | tf_op jit(solution)/shard_map/all_to_all | solution.py:111
  229.2 56.1 %all-gather.2.cloned.1.call-done = bf16[768,4,768]{2,0,1:T(8,128)(2,1)} async-done(((bf16[192,4,768]{2,0,1:T(8,128)(2,1)}), bf16[768,4,768]{2,0,1:T(8,128)(2,1)}) %all-gather.2.cloned.1.call-update) | async-done | bytes 4718608 | tf_op jit(solution)/shard_map/all_gather | solution.py:95
  285.3 4.5 %fusion.46 = bf16[192,4,768]{2,0,1:T(8,128)(2,1)} fusion(bf16[768,4,768]{2,0,1:T(8,128)(2,1)} %all-gather.2.cloned.1.call-done, bf16[192,4,768]{0,2,1:T(8,128)(2,1)S(1)} %bitcast.90), kind=kOutput, calls=%fused_computation.66 | convolution fusion | flops 906559488 | bytes 7077888 | tf_op jit(solution)/shard_map/icj,jck->ick/dot_general | solution.py:92
  289.8 3.6 copy.67
  293.4 10.1 %all-to-all-start.2 = ((bf16[192,4,768]{0,1,2:T(4,128)(2,1)}), bf16[192,4,768]{0,1,2:T(4,128)(2,1)}, u32[]{:S(2)}, u32[]{:S(2)}) async-start(bf16[192,4,768]{0,1,2:T(4,128)(2,1)} %copy.67), calls=%async_computation.2 | async-start | bytes 3145728 | tf_op jit(solution)/shard_map/all_to_all | solution.py:108
  308.1 19.1 %all-to-all-done.2 = bf16[192,4,768]{0,1,2:T(4,128)(2,1)} async-done(((bf16[192,4,768]{0,1,2:T(4,128)(2,1)}), bf16[192,4,768]{0,1,2:T(4,128)(2,1)}, u32[]{:S(2)}, u32[]{:S(2)}) %all-to-all-start.2) | async-done | bytes 1179680 | tf_op jit(solution)/shard_map/all_to_all | solution.py:108
  331.3 3.3 copy.71
  334.6 2.9 fusion.50
  337.7 3.0 fusion.49
  343.1 3.2 fusion.51
  346.3 4.1 %fusion.45 = bf16[192,24,640]{2,1,0:T(8,128)(2,1)S(1)} fusion(bf16[192,24,640]{2,1,0:T(8,128)(2,1)S(1)} %fusion.51, bf16[192,24,128]{2,1,0:T(8,128)(2,1)S(1)} %copy-done.18, bf16[192,24,128]{2,1,0:T(8,128)(2,1)S(1)} %copy-done.6, f32[128]{0:T(128)S(1)} %copy-done.20, f32[128]{0:T(128)S(1)} %copy-done.16, f32[192,24]{1,0:T(8,128)S(1)} %copy-done.13, ...), kind=kOutput, calls=%fused_computation.64 | convolution fusion | flops 159842304 | bytes 6128640 | tf_op jit(solution)/shard_map/ikc,cd->ikd/dot_general | solution.py:72
  353.1 4.0 %fusion.22 = bf16[192,24,128]{2,1,0:T(8,128)(2,1)} fusion(bf16[192,24,128]{2,1,0:T(8,128)(2,1)S(1)} %copy-done.4, f32[192,24,128]{2,1,0:T(8,128)S(1)} %get-tuple-element.12, f32[192,24]{1,0:T(8,128)S(1)} %broadcast_multiply_fusion, f32[192,24]{1,0:T(8,128)S(1)} %broadcast_multiply_fusion.1, f32[128]{0:T(128)S(1)} %copy-done.14, f32[192,24]{1,0:T(8,128)S(1)} %copy-done.9, ...), kind=kLoop, calls=%fused_computation.30 | loop fusion | flops 5308416 | bytes 4792832 | tf_op jit(solution)/shard_map/convert_element_type | solution.py:130
  (83 shorter events, 43.0 us)
Async XLA Ops:
  6.5 8.4 %copy-start = (bf16[128,640]{1,0:T(8,128)(2,1)S(1)}, bf16[128,640]{1,0:T(8,128)(2,1)}, u32[]{:S(2)}) copy-start(bf16[128,640]{1,0:T(8,128)(2,1)} %param.18) | copy-start | bytes 491524
  6.5 6.3 %copy-start.3 = (bf16[192,24,128]{2,1,0:T(8,128)(2,1)S(1)}, bf16[192,24,128]{2,1,0:T(8,128)(2,1)}, u32[]{:S(2)}) copy-start(bf16[192,24,128]{2,1,0:T(8,128)(2,1)} %param.12) | copy-start | bytes 3538948
  6.5 8.4 %copy-start.14 = (f32[128]{0:T(128)S(1)}, f32[128]{0:T(128)}, u32[]{:S(2)}) copy-start(f32[128]{0:T(128)} %param.20) | copy-start | bytes 1540
  6.5 8.4 %copy-start.15 = (f32[128]{0:T(128)S(1)}, f32[128]{0:T(128)}, u32[]{:S(2)}) copy-start(f32[128]{0:T(128)} %param.21) | copy-start | bytes 1540
  17.7 4.7 %copy-start.1 = (f32[192,24,640]{2,1,0:T(8,128)}, f32[192,24,640]{2,1,0:T(8,128)S(1)}, u32[]{:S(2)}) copy-start(f32[192,24,640]{2,1,0:T(8,128)S(1)} %fusion.55) | copy-start | bytes 35389444
  22.5 13.7 %copy-start.5 = (bf16[192,24,128]{2,1,0:T(8,128)(2,1)S(1)}, bf16[192,24,128]{2,1,0:T(8,128)(2,1)}, u32[]{:S(2)}) copy-start(bf16[192,24,128]{2,1,0:T(8,128)(2,1)} %param.13) | copy-start | bytes 3538948
  24.9 13.5 %copy-start.16 = (f32[128]{0:T(128)S(1)}, f32[128]{0:T(128)}, u32[]{:S(2)}) copy-start(f32[128]{0:T(128)} %param.22) | copy-start | bytes 1540
  24.9 13.5 %copy-start.19 = (bf16[128,128]{1,0:T(8,128)(2,1)S(1)}, bf16[128,128]{1,0:T(8,128)(2,1)}, u32[]{:S(2)}) copy-start(bf16[128,128]{1,0:T(8,128)(2,1)} %param.19) | copy-start | bytes 98308
  24.9 34.5 %all-to-all-start.3 = ((bf16[192,128,24]{0,2,1:T(8,128)(2,1)}), bf16[192,128,24]{0,2,1:T(8,128)(2,1)S(1)}, u32[]{:S(2)}, u32[]{:S(2)}) async-start(bf16[192,128,24]{0,2,1:T(8,128)(2,1)} %copy.72), calls=%async_computation.3 | async-start | bytes 3145728 | tf_op jit(solution)/shard_map/all_to_all | solution.py:88
  36.9 6.0 %copy-start.10 = (f32[192,24]{1,0:T(8,128)}, f32[192,24]{1,0:T(8,128)S(1)}, u32[]{:S(2)}) copy-start(f32[192,24]{1,0:T(8,128)S(1)} %broadcast_multiply_fusion.4) | copy-start | bytes 55300
  38.4 4.5 %copy-start.12 = (f32[192,24]{1,0:T(8,128)}, f32[192,24]{1,0:T(8,128)S(1)}, u32[]{:S(2)}) copy-start(f32[192,24]{1,0:T(8,128)S(1)} %add_rsqrt_fusion) | copy-start | bytes 55300
  59.3 26.1 %all-to-all-start.1 = ((bf16[192,128,24]{0,2,1:T(8,128)(2,1)}), bf16[192,128,24]{0,2,1:T(8,128)(2,1)}, u32[]{:S(2)}, u32[]{:S(2)}) async-start(bf16[192,128,24]{0,2,1:T(8,128)(2,1)} %copy.64), calls=%async_computation.1 | async-start | bytes 3145728 | tf_op jit(solution)/shard_map/all_to_all | solution.py:87
  64.0 151.8 %all-reduce.3.cloned.1.call-start = ((), (), s32[]{:S(2)}) async-start(), calls=%async_computation.6 | async-start | bytes 9437184
  65.4 21.6 %copy-start.7 = (bf16[192,4,32,24]{0,3,2,1:T(8,128)(2,1)S(1)}, bf16[192,4,32,24]{0,3,2,1:T(8,128)(2,1)}, u32[]{:S(2)}) copy-start(bf16[192,4,32,24]{0,3,2,1:T(8,128)(2,1)} %copy.73) | copy-start | bytes 3538948
  99.1 186.2 %all-gather.2.cloned.1.call-start = ((), (), s32[]{:S(2)}) async-start(), calls=%async_computation.5 | async-start | bytes 5898240 | tf_op jit(solution)/shard_map/all_gather | solution.py:95
  220.1 73.3 %all-to-all-start.4 = ((bf16[192,4,768]{0,1,2:T(4,128)(2,1)}), bf16[192,4,768]{0,1,2:T(4,128)(2,1)S(1)}, u32[]{:S(2)}, u32[]{:S(2)}) async-start(bf16[192,4,768]{0,1,2:T(4,128)(2,1)} %copy.77), calls=%async_computation.4 | async-start | bytes 3145728 | tf_op jit(solution)/shard_map/all_to_all | solution.py:111
  293.4 33.9 %all-to-all-start.2 = ((bf16[192,4,768]{0,1,2:T(4,128)(2,1)}), bf16[192,4,768]{0,1,2:T(4,128)(2,1)}, u32[]{:S(2)}, u32[]{:S(2)}) async-start(bf16[192,4,768]{0,1,2:T(4,128)(2,1)} %copy.67), calls=%async_computation.2 | async-start | bytes 3145728 | tf_op jit(solution)/shard_map/all_to_all | solution.py:108
  343.0 3.2 copy-start.6
  343.1 3.2 copy-start.11
  343.1 3.2 copy-start.13
  343.1 3.2 copy-start.18
  343.1 3.2 copy-start.20
  346.3 4.2 %copy-start.4 = (bf16[192,24,128]{2,1,0:T(8,128)(2,1)S(1)}, bf16[192,24,128]{2,1,0:T(8,128)(2,1)}, u32[]{:S(2)}) copy-start(bf16[192,24,128]{2,1,0:T(8,128)(2,1)} %param.12) | copy-start | bytes 3538948
  346.3 4.2 %copy-start.9 = (f32[192,24]{1,0:T(8,128)S(1)}, f32[192,24]{1,0:T(8,128)}, u32[]{:S(2)}) copy-start(f32[192,24]{1,0:T(8,128)} %copy-done.8) | copy-start | bytes 55300
  (4 other events, 7.5 us)
Sparse Core Ops, SparseCore 0:
  99.2 116.6 all-reduce.2
  217.5 67.7 all-gather.1
where the time goes:
time: 365 us; the launch traced here: 364 us
  waiting for transfers between devices  187 us (51%)
  local copies, waits for them, and re-layouts  45.2 us (12%)
  starting transfers between devices  35.5 us (10%)
  other arithmetic  30.3 us (8%)
  blocking collectives  28.1 us (8%)
  matrix products  23 us (6%)
  between operations  14.5 us (4%)
    unnamed x3, waiting for transfers between devices  82.9 us
    all_gather x1, waiting for transfers between devices, on_device(): lax.all_gather(right_ch, 'half', axis=0, tiled=True)  56.1 us
    all_to_all x1, blocking collectives, on_device(): lax.all_to_all(outgoing[2], 'ch', split_axis=1, concat_axis=2, tiled=True)  28.1 us
    all_to_all x1, waiting for transfers between devices, on_device(): lax.all_to_all(outgoing[0], 'ch', split_axis=1, concat_axis=2, tiled=True)  20.1 us
    all_to_all x1, waiting for transfers between devices, on_device(): lax.all_to_all(grad_left.astype(jnp.bfloat16), 'ch', split_axis=2, concat...  19.1 us
    unnamed x4, other arithmetic  11.4 us
    all_to_all x1, starting transfers between devices, on_device(): lax.all_to_all(outgoing[1], 'ch', split_axis=1, concat_axis=2, tiled=True)  11.3 us
    all_to_all x1, starting transfers between devices, on_device(): lax.all_to_all(grad_left.astype(jnp.bfloat16), 'ch', split_axis=2, concat...  10.1 us
  transfers between devices with their start and end apart: 6, of which 5 were waited for; matrix products, arithmetic and copies ran while one was open for 10% of the time, Pallas kernels for 0%

commit v1 on v0

v1 whole, which is shorter than its diff:
```python
import functools

import jax
import jax.numpy as jnp
from jax import lax
from jax.experimental import pallas as pl
from jax.experimental.pallas import tpu as pltpu
from jax.sharding import PartitionSpec as P

EPSILON = 1e-05
AXES = ("ch", "half")
F32 = jnp.float32
BF16 = jnp.bfloat16

ROWS, COLS, C = 192, 24, 128
HALF_COLS = COLS // 2
OUT_ROWS = 112
BACK_ROWS = 72
G_A, G_B, L_A, R_A, LR_B = 0, 24, 40, 64, 88
RES = 768


def dot(a, b):
    return jnp.dot(a, b, preferred_element_type=F32)


def sigmoid(x):
    return 0.5 * jnp.tanh(0.5 * x) + 0.5


def unit(x):
    centred = x - jnp.mean(x, 0, keepdims=True)
    inv = lax.rsqrt(jnp.mean(centred * centred, 0, keepdims=True) + EPSILON)
    return centred * inv, inv


def norm_back(grad, unit_val, inv):
    first = jnp.mean(grad, 0, keepdims=True)
    second = jnp.mean(grad * unit_val, 0, keepdims=True)
    return inv * (grad - first - unit_val * second)


def tile3(x):
    return jnp.concatenate([x, x, x], 1)


def column(row):
    return jnp.broadcast_to(row, (C, C)).T


def swap(x):
    return pltpu.roll(x, 64, 1)


def low_lanes(shape):
    return lax.broadcasted_iota(jnp.int32, shape, 1) < 64


def spread(src, dst):
    def body(i, _):
        at = pl.multiple_of(i * 8, 8)
        dst[pl.ds(pl.multiple_of(i * 192, 8), 192), :] = src[pl.ds(at, 8)].astype(F32).reshape(192, C)
        return 0

    lax.fori_loop(0, ROWS // 8, body, 0)


def gather_cols(src, q):
    base = C * COLS
    parts = [
        src[pl.ds(q, C, stride=COLS), :],
        src[pl.ds(q + HALF_COLS, C, stride=COLS), :],
        src[pl.ds(base + q, 64, stride=COLS), :],
        src[pl.ds(base + q + HALF_COLS, 64, stride=COLS), :],
    ]
    return jnp.concatenate(parts, 0).T


def row_code(mask_ref, chain_ref):
    half = lax.axis_index("half")
    code = jnp.where(mask_ref[...] > 0, chain_ref[...], -1)
    code = jnp.broadcast_to(code, (8, RES))
    code = pltpu.roll(code, lax.rem(RES - half * ROWS, RES), 1)[:1]
    low = code[:, C : C + C]
    return code[:, :C], jnp.where(low_lanes((1, C)), low, swap(low))


def keep_row(q, codes, mask_s, chain_s, pairs_s):
    first = lax.axis_index("ch") * COLS + q
    factors = []
    for k in (first, first + HALF_COLS):
        chain = chain_s[k]
        factors.append([(pairs_s[c, chain] * mask_s[k]).astype(F32) for c in range(4)])

    def pick(code, factor):
        out = jnp.zeros(code.shape, F32)
        for c in range(4):
            out = jnp.where(code == c, factor[c], out)
        return out

    code_a, code_b = codes
    tail = jnp.where(low_lanes((1, C)), pick(code_b, factors[0]), pick(code_b, factors[1]))
    return jnp.concatenate([pick(code_a, factors[0]), pick(code_a, factors[1]), tail], 1)


def prepare(w_ref, wo_ref, gains, wt, wot, cols):
    wt[...] = w_ref[...].astype(F32).T.astype(BF16)
    wot[...] = wo_ref[...].astype(F32).T.astype(BF16)
    for n, g in enumerate(gains):
        cols[n] = column(g[...])


def front_kernel(
    pair_ref, tri_ref, cot_ref, mask_v, chain_v, mask_s, chain_s, pairs_s,
    w_ref, wo_ref, in_gain, in_bias, out_gain, out_bias, out_ref,
    xp, xt, xc, wt, wot, cols, stage,
):
    prepare(w_ref, wo_ref, (in_gain, in_bias, out_gain, out_bias), wt, wot, cols)
    spread(pair_ref, xp)
    spread(tri_ref, xt)
    spread(cot_ref, xc)
    codes = row_code(mask_v, chain_v)

    def put(row, value):
        stage[pl.ds(row, C, stride=OUT_ROWS), :] = value

    for r in range(4):
        put(36 + r, jnp.zeros((C, C), F32))

    def body(q, _):
        keep = keep_row(q, codes, mask_s, chain_s, pairs_s)
        z, _ = unit(gather_cols(xp, q))
        nz = (z * tile3(cols[0]) + tile3(cols[1])).astype(BF16)
        proj = dot(wt[...], nz)
        left = keep * sigmoid(proj[C : 2 * C]) * proj[:C]
        right = keep * sigmoid(proj[3 * C : 4 * C]) * proj[2 * C : 3 * C]
        outer = (gather_cols(xc, q) * sigmoid(proj[4 * C :])).astype(BF16)
        u, inv = unit(gather_cols(xt, q))
        grad = norm_back(dot(wo_ref[...], outer) * tile3(cols[2]), u, inv)
        put(G_A + q, grad[:, :C])
        put(G_A + HALF_COLS + q, grad[:, C : 2 * C])
        put(G_B + q, grad[:, 2 * C :])
        put(L_A + q, left[:, :C])
        put(L_A + HALF_COLS + q, left[:, C : 2 * C])
        put(R_A + q, right[:, :C])
        put(R_A + HALF_COLS + q, right[:, C : 2 * C])
        low = low_lanes((C, C))
        tail_l, tail_r = left[:, 2 * C :], right[:, 2 * C :]
        put(LR_B + q, jnp.where(low, tail_l, swap(tail_r)))
        put(LR_B + HALF_COLS + q, jnp.where(low, swap(tail_l), tail_r))
        return 0

    lax.fori_loop(0, HALF_COLS, body, 0)

    def flush(c, _):
        at = pl.multiple_of(c * OUT_ROWS, 8)
        out_ref[c] = stage[pl.ds(at, OUT_ROWS), :].astype(BF16)
        return 0

    lax.fori_loop(0, C, flush, 0)


def save_kernel(
    pair_ref, tri_ref, cot_ref, mask_v, chain_v, mask_s, chain_s, pairs_s,
    w_ref, wo_ref, in_gain, in_bias, out_gain, out_bias, saved_ref, inv_ref,
    xp, xt, xc, wt, wot, cols,
):
    prepare(w_ref, wo_ref, (in_gain, in_bias, out_gain, out_bias), wt, wot, cols)
    spread(pair_ref, xp)
    spread(tri_ref, xt)
    spread(cot_ref, xc)
    codes = row_code(mask_v, chain_v)

    def body(q, _):
        keep = keep_row(q, codes, mask_s, chain_s, pairs_s)
        z, inv_z = unit(gather_cols(xp, q))
        nz = (z * tile3(cols[0]) + tile3(cols[1])).astype(BF16)
        proj = dot(wt[...], nz)
        gate_l = sigmoid(proj[C : 2 * C])
        gate_r = sigmoid(proj[3 * C : 4 * C])
        gate_o = sigmoid(proj[4 * C :])
        u, _ = unit(gather_cols(xt, q))
        nx = (u * tile3(cols[2]) + tile3(cols[3])).astype(BF16)
        out_proj = dot(wot[...], nx)
        keep_l, keep_r = keep * gate_l, keep * gate_r
        saved_ref[q, 0] = keep_l.astype(BF16)
        saved_ref[q, 1] = (keep_l * proj[:C] * (1.0 - gate_l)).astype(BF16)
        saved_ref[q, 2] = keep_r.astype(BF16)
        saved_ref[q, 3] = (keep_r * proj[2 * C : 3 * C] * (1.0 - gate_r)).astype(BF16)
        saved_ref[q, 4] = (gather_cols(xc, q) * out_proj * gate_o * (1.0 - gate_o)).astype(BF16)
        saved_ref[q, 5] = z.astype(BF16)
        inv_ref[q] = jnp.broadcast_to(inv_z, (8, 3 * C))
        return 0

    lax.fori_loop(0, HALF_COLS, body, 0)


def channel_kernel(in_ref, out_ref, g, left, right, back_l, back_r):
    low24 = low_lanes((COLS, C))
    low12 = low_lanes((HALF_COLS, C))

    def take(w):
        blocks = [in_ref[w * 4 + h].astype(F32) for h in range(4)]
        rows_g = [b[G_A : G_A + COLS] for b in blocks]
        rows_l = [b[L_A : L_A + COLS] for b in blocks]
        rows_r = [b[R_A : R_A + COLS] for b in blocks]
        for h in (0, 2):
            a, b = blocks[h][G_B : G_B + HALF_COLS], blocks[h + 1][G_B : G_B + HALF_COLS]
            rows_g.append(jnp.concatenate([jnp.where(low12, a, swap(b)), jnp.where(low12, swap(a), b)], 0))
            a, b = blocks[h][LR_B : LR_B + COLS], blocks[h + 1][LR_B : LR_B + COLS]
            rows_l.append(jnp.where(low24, a, swap(b)))
            rows_r.append(jnp.where(low24, swap(a), b))
        return [jnp.concatenate(rows, 1) for rows in (rows_g, rows_l, rows_r)]

    def gather(pair, _):
        one, two = take(2 * pair), take(2 * pair + 1)
        at = pl.ds(pl.multiple_of(pair * 48, 16), 48)
        for ref, a, b in zip((g, left, right), one, two):
            ref[at, :] = jnp.concatenate([a, b], 0).astype(BF16)
        return 0

    lax.fori_loop(0, 16, gather, 0)
    spans = [(ROWS * h, C) for h in range(4)] + [(ROWS * h + C, 64) for h in range(4)]
    ordered = jnp.concatenate([g[at : at + size, :] for at, size in spans], 0)
    back_l[...] = dot(right[...], ordered)
    back_r[...] = lax.dot_general(left[...], ordered, (((1,), (1,)), ((), ())), preferred_element_type=F32)

    def give(w, _):
        at = pl.ds(pl.multiple_of(w * COLS, 8), COLS)
        for h in range(4):
            lanes = slice(h * C, (h + 1) * C)
            tail = slice((4 + h // 2) * C, (5 + h // 2) * C)
            a, b = back_l[at, tail], back_r[at, tail]
            mixed = jnp.where(low24, a, swap(b)) if h % 2 == 0 else jnp.where(low24, swap(a), b)
            out_ref[w * 4 + h] = jnp.concatenate([back_l[at, lanes], back_r[at, lanes], mixed], 0).astype(BF16)
        return 0

    lax.fori_loop(0, 32, give, 0)


def back_kernel(in_ref, saved_ref, inv_ref, w_ref, in_gain, out_ref, rows, cols, stage):
    cols[...] = column(in_gain[...])

    def fill(c, _):
        at = pl.multiple_of(c * BACK_ROWS, 8)
        rows[pl.ds(at, BACK_ROWS), :] = in_ref[c].astype(F32)
        return 0

    lax.fori_loop(0, C, fill, 0)

    def body(q, _):
        low = low_lanes((C, C))

        def get(row):
            return rows[pl.ds(row, C, stride=BACK_ROWS), :]

        a, b = get(48 + q), get(48 + HALF_COLS + q)
        tail_l = jnp.where(low, a, swap(b))
        tail_r = jnp.where(low, swap(a), b)
        grad_l = jnp.concatenate([get(q), get(HALF_COLS + q), tail_l], 1)
        grad_r = jnp.concatenate([get(COLS + q), get(COLS + HALF_COLS + q), tail_r], 1)
        grad_proj = jnp.concatenate(
            [
                (grad_l * saved_ref[q, 0].astype(F32)).astype(BF16),
                (grad_l * saved_ref[q, 1].astype(F32)).astype(BF16),
                (grad_r * saved_ref[q, 2].astype(F32)).astype(BF16),
                (grad_r * saved_ref[q, 3].astype(F32)).astype(BF16),
                saved_ref[q, 4],
            ],
            0,
        )
        e = dot(w_ref[...], grad_proj) * tile3(cols[...])
        grad = norm_back(e, saved_ref[q, 5].astype(F32), inv_ref[q][:1]).T
        base = C * COLS
        stage[pl.ds(q, C, stride=COLS), :] = grad[:C]
        stage[pl.ds(q + HALF_COLS, C, stride=COLS), :] = grad[C : 2 * C]
        stage[pl.ds(base + q, 64, stride=COLS), :] = grad[2 * C : 2 * C + 64]
        stage[pl.ds(base + q + HALF_COLS, 64, stride=COLS), :] = grad[2 * C + 64 :]
        return 0

    lax.fori_loop(0, HALF_COLS, body, 0)

    def flush(i, _):
        at = pl.multiple_of(i * 8, 8)
        rows8 = stage[pl.ds(pl.multiple_of(i * 192, 8), 192), :].reshape(8, COLS, C)
        out_ref[pl.ds(at, 8)] = rows8.astype(BF16)
        return 0

    lax.fori_loop(0, ROWS // 8, flush, 0)


def call(kernel, outs, scratch, args, smem=(), flops=0, moved=0, limit=30):
    vmem, scal = pl.BlockSpec(memory_space=pltpu.VMEM), pl.BlockSpec(memory_space=pltpu.SMEM)
    single = not isinstance(outs, tuple)
    return pl.pallas_call(
        kernel,
        out_shape=outs,
        in_specs=[scal if n in smem else vmem for n in range(len(args))],
        out_specs=vmem if single else tuple(vmem for _ in outs),
        scratch_shapes=scratch,
        compiler_params=pltpu.CompilerParams(vmem_limit_bytes=limit << 20),
        cost_estimate=pl.CostEstimate(flops=flops, bytes_accessed=moved, transcendentals=0),
    )(*args)


def exchange(x):
    return lax.all_to_all(x, AXES, split_axis=0, concat_axis=0, tiled=True)


def on_device(
    pair_act,
    tri_out,
    cotangent,
    residue_mask,
    chain_index,
    chain_pairs,
    in_weight,
    out_weight,
    in_gain,
    in_bias,
    out_gain,
    out_bias,
):
    shape = jax.ShapeDtypeStruct
    gains = [g.reshape(1, C) for g in (in_gain, in_bias, out_gain, out_bias)]
    given = [
        pair_act, tri_out, cotangent, residue_mask.reshape(1, RES), chain_index.reshape(1, RES),
        residue_mask, chain_index, chain_pairs, in_weight, out_weight, *gains,
    ]
    smem = (5, 6, 7)
    tile = pltpu.VMEM((ROWS * COLS, C), F32)
    shared = [tile, tile, tile, pltpu.VMEM((5 * C, C), BF16), pltpu.VMEM((C, C), BF16), pltpu.VMEM((4, C, C), F32)]
    sent = call(
        front_kernel,
        shape((C, OUT_ROWS, C), BF16),
        shared + [pltpu.VMEM((C * OUT_ROWS, C), F32)],
        given,
        smem,
        flops=2 * 4608 * 128 * 768,
        moved=8 << 20,
    )
    saved, inv = call(
        save_kernel,
        (shape((HALF_COLS, 6, C, 3 * C), BF16), shape((HALF_COLS, 8, 3 * C), F32)),
        shared,
        given,
        smem,
        flops=2 * 4608 * 128 * 768,
        moved=12 << 20,
    )
    got = exchange(sent)
    square = pltpu.VMEM((RES, RES), BF16)
    wide = pltpu.VMEM((RES, RES), F32)
    back = call(
        channel_kernel,
        shape((C, BACK_ROWS, C), BF16),
        [square, square, square, wide, wide],
        [got],
        flops=4 * RES**3,
        moved=8 << 20,
    )
    returned = exchange(back)
    return call(
        back_kernel,
        shape((ROWS, COLS, C), BF16),
        [pltpu.VMEM((C * BACK_ROWS, C), F32), pltpu.VMEM((C, C), F32), tile],
        [returned, saved, inv, in_weight, gains[0]],
        flops=2 * 4608 * 128 * 640,
        moved=12 << 20,
    )


def solution(mesh):
    return jax.shard_map(
        on_device,
        mesh=mesh,
        in_specs=(P("half", "ch", None),) * 3 + (P(),) * 9,
        out_specs=P("half", "ch", None),
        check_vma=False,
    )
```

time: 365 us -> 142 us (0.39)
  waiting for transfers between devices: 187 us -> 14.2 us
  Pallas kernels: 0 us -> 34.3 us
  starting transfers between devices: 35.5 us -> 4.62 us
  blocking collectives: 28.1 us -> 58.8 us
  other arithmetic: 30.3 us -> 0 us
  matrix products: 23 us -> 0 us
  local copies, waits for them, and re-layouts: 45.2 us -> 29.5 us
  between operations: 14.5 us -> 0.1 us
    unnamed x3 -> x0, waiting for transfers between devices: 82.9 us -> none
    all_gather x1 -> x0, waiting for transfers between devices: 56.1 us -> none  [on_device(): lax.all_gather(right_ch, 'half', axis=0, tiled=True)]
    pallas_call x0 -> x4, Pallas kernels: none -> 34.3 us  [call(): pl.pallas_call(kernel, out_shape=outs, in_specs=[scal if n in smem else v...]
    all_to_all x4 -> x1, waiting for transfers between devices: 48.3 us -> 14.2 us  [exchange(): return lax.all_to_all(x, AXES, split_axis=0, concat_axis=0, tiled=True)]
    all_to_all x1, blocking collectives: 28.1 us -> 58.8 us  [exchange(): return lax.all_to_all(x, AXES, split_axis=0, concat_axis=0, tiled=True)]
    all_to_all x4 -> x1, starting transfers between devices: 35.2 us -> 4.62 us  [exchange(): return lax.all_to_all(x, AXES, split_axis=0, concat_axis=0, tiled=True)]
    unnamed x46 -> x62, local copies, waits for them, and re-layouts: 4.51 us -> 28.2 us
    dot_general x7 -> x0, matrix products: 23 us -> none  [the longest x1 4.48 us: on_device(): jnp.einsum('icj,jck->ick', grad_block, lax.all_gather(right_ch, 'half', a...]
  transfers between devices with their start and end apart: 6 -> 1, of which waited for: 5 -> 1; matrix products, arithmetic and copies ran while one was open for 10% -> 0% of each run, Pallas kernels for 0% -> 6%
where the time goes in v1:
time: 142 us
  blocking collectives  58.8 us (41%)
  Pallas kernels  34.3 us (24%)
  local copies, waits for them, and re-layouts  29.5 us (21%)
  waiting for transfers between devices  14.2 us (10%)
  starting transfers between devices  4.62 us (3%)
    all_to_all x1, blocking collectives, exchange(): return lax.all_to_all(x, AXES, split_axis=0, concat_axis=0, tiled=True)  58.8 us
    pallas_call x4, Pallas kernels, call(): pl.pallas_call(kernel, out_shape=outs, in_specs=[scal if n in smem else v...  34.3 us
    unnamed x62, local copies, waits for them, and re-layouts  28.2 us
    all_to_all x1, waiting for transfers between devices, exchange(): return lax.all_to_all(x, AXES, split_axis=0, concat_axis=0, tiled=True)  14.2 us
    all_to_all x1, starting transfers between devices, exchange(): return lax.all_to_all(x, AXES, split_axis=0, concat_axis=0, tiled=True)  4.62 us
  transfers between devices with their start and end apart: 1, of which 1 were waited for; matrix products, arithmetic and copies ran while one was open for 0% of the time, Pallas kernels for 6%

profile of v1, /device:TPU:1, one launch (start us, length us, event | category | flops | bytes accessed | tf_op | source)
XLA Modules:
  0.0 141.5 jit_solution(17888596320839108275)
XLA Ops:
  0.0 0.7 reshape.18.mask_v
  0.7 0.7 reshape.19.chain_v
  1.4 1.3 copy-done.2
  2.7 1.3 copy-done.4
  3.9 1.3 copy-done.6
  5.2 0.9 copy-done.9
  6.1 0.8 copy-done.14
  6.9 0.7 copy-done.16
  11.5 12.5 %shard_map.118 = bf16[128,112,128]{2,1,0:T(8,128)(2,1)S(1)} custom-call(bf16[192,24,128]{2,1,0:T(8,128)(2,1)S(1)} %copy-done.2, bf16[192,24,128]{2,1,0:T(8,128)(2,1)S(1)} %copy-done.4, bf16[192,24,128]{2,1,0:T(8,128)(2,1)S(1)} %copy-done.6, s32[1,768]{1,0:T(1,128)S(1)} %reshape.18.mask_v, s32[1,768]{1,0:T(1,128)S(1)} %reshape.19.chain_v, ...), custom_call_target="tpu_custom_call" | custom-call | flops 905969664 | bytes 8388608 | tf_op jit(solution)/shard_map/pallas_call | solution.py:295
  24.1 58.8 %all_to_all.10.in_ref = bf16[128,112,128]{2,1,0:T(8,128)(2,1)S(1)} all-to-all(bf16[128,112,128]{2,1,0:T(8,128)(2,1)S(1)} %shard_map.118), channel_id=1, replica_groups=mesh['ch'=32,'half'=4] {'ch','half'}, dimensions={0} | all-to-all | bytes 7340032 | tf_op jit(solution)/shard_map/all_to_all | solution.py:307
  82.9 5.9 %shard_map.119 = bf16[128,72,128]{2,1,0:T(8,128)(2,1)S(1)} custom-call(bf16[128,112,128]{2,1,0:T(8,128)(2,1)S(1)} %all_to_all.10.in_ref), custom_call_target="tpu_custom_call" | custom-call | flops 1811939328 | bytes 8388608 | tf_op jit(solution)/shard_map/pallas_call | solution.py:295
  88.9 1.5 %copy-done.8 = bf16[128,72,128]{2,1,0:T(8,128)(2,1)} copy-done((bf16[128,72,128]{2,1,0:T(8,128)(2,1)}, bf16[128,72,128]{2,1,0:T(8,128)(2,1)S(1)}, u32[]{:S(2)}) %copy-start.8) | copy-done | bytes 2359320
  90.4 4.6 %all-to-all-start.1 = ((bf16[128,72,128]{2,1,0:T(8,128)(2,1)}), bf16[128,72,128]{2,1,0:T(8,128)(2,1)S(1)}, u32[]{:S(2)}, u32[]{:S(2)}) async-start(bf16[128,72,128]{2,1,0:T(8,128)(2,1)} %copy-done.8), calls=%async_computation.1 | async-start | bytes 4718592 | tf_op jit(solution)/shard_map/all_to_all | solution.py:307
  95.0 1.3 copy-done.5
  96.3 1.3 copy-done.7
  97.6 0.9 copy-done.10
  98.5 0.8 copy-done.15
  102.5 8.2 %shard_map.120 = (bf16[12,6,128,384]{3,2,1,0:T(8,128)(2,1)S(1)}, f32[12,8,384]{2,1,0:T(8,128)S(1)}) custom-call(bf16[192,24,128]{2,1,0:T(8,128)(2,1)S(1)} %copy-done.3, bf16[192,24,128]{2,1,0:T(8,128)(2,1)S(1)} %copy-done.5, bf16[192,24,128]{2,1,0:T(8,128)(2,1)S(1)} %copy-done.7, s32[1,768]{1,0:T(1,128)S(1)} %reshape.18.mask_v, ...), custom_call_target="tpu_custom_call" | custom-call | flops 905969664 | bytes 12582912 | tf_op jit(solution)/shard_map/pallas_call | solution.py:295
  110.7 2.9 %copy-done = bf16[12,6,128,384]{3,2,1,0:T(8,128)(2,1)} copy-done((bf16[12,6,128,384]{3,2,1,0:T(8,128)(2,1)}, bf16[12,6,128,384]{3,2,1,0:T(8,128)(2,1)S(1)}, u32[]{:S(2)}) %copy-start) | copy-done | bytes 7077912
  114.3 14.2 %all-to-all-done.1.in_ref = bf16[128,72,128]{2,1,0:T(8,128)(2,1)S(1)} async-done(((bf16[128,72,128]{2,1,0:T(8,128)(2,1)}), bf16[128,72,128]{2,1,0:T(8,128)(2,1)S(1)}, u32[]{:S(2)}, u32[]{:S(2)}) %all-to-all-start.1) | async-done | bytes 2359328 | tf_op jit(solution)/shard_map/all_to_all | solution.py:307
  128.4 3.0 %copy-done.1 = bf16[12,6,128,384]{3,2,1,0:T(8,128)(2,1)S(1)} copy-done((bf16[12,6,128,384]{3,2,1,0:T(8,128)(2,1)S(1)}, bf16[12,6,128,384]{3,2,1,0:T(8,128)(2,1)}, u32[]{:S(2)}) %copy-start.1) | copy-done | bytes 7077912
  131.4 0.9 copy-done.11
  132.4 0.9 copy-done.13
  133.9 7.6 %shard_map.121 = bf16[192,24,128]{2,1,0:T(8,128)(2,1)} custom-call(bf16[128,72,128]{2,1,0:T(8,128)(2,1)S(1)} %all-to-all-done.1.in_ref, bf16[12,6,128,384]{3,2,1,0:T(8,128)(2,1)S(1)} %copy-done.1, f32[12,8,384]{2,1,0:T(8,128)S(1)} %copy-done.13, bf16[128,640]{1,0:T(8,128)(2,1)S(1)} %copy-done.11, f32[1,128]{1,0:T(1,128)S(1)} %bitcast.6), custom_call_target="tpu_custom_call" | custom-call | flops 754974720 | bytes 12582912 | tf_op jit(solution)/shard_map/pallas_call | solution.py:295
  (47 shorter events, 8.6 us)
Async XLA Ops:
  1.4 1.3 copy-start.2
  2.7 1.3 copy-start.4
  3.9 1.3 copy-start.6
  5.2 0.9 copy-start.9
  6.1 0.8 copy-start.14
  6.9 0.7 copy-start.16
  7.6 0.7 copy-start.18
  8.2 0.7 copy-start.20
  10.2 0.7 copy-start.27
  88.9 1.5 %copy-start.8 = (bf16[128,72,128]{2,1,0:T(8,128)(2,1)}, bf16[128,72,128]{2,1,0:T(8,128)(2,1)S(1)}, u32[]{:S(2)}) copy-start(bf16[128,72,128]{2,1,0:T(8,128)(2,1)S(1)} %shard_map.119) | copy-start | bytes 7077892
  90.3 4.6 %copy-start.3 = (bf16[192,24,128]{2,1,0:T(8,128)(2,1)S(1)}, bf16[192,24,128]{2,1,0:T(8,128)(2,1)}, u32[]{:S(2)}) copy-start(bf16[192,24,128]{2,1,0:T(8,128)(2,1)} %pair_ref.3) | copy-start | bytes 3538948
  90.3 4.6 %copy-start.17 = (s32[768]{0:T(1024)S(1)}, s32[768]{0:T(1024)}, u32[]{:S(2)}) copy-start(s32[768]{0:T(1024)} %mask_s.3) | copy-start | bytes 9220
  90.4 4.6 %copy-start.19 = (s32[768]{0:T(1024)S(1)}, s32[768]{0:T(1024)}, u32[]{:S(2)}) copy-start(s32[768]{0:T(1024)} %chain_s.3) | copy-start | bytes 9220
  90.4 38.1 %all-to-all-start.1 = ((bf16[128,72,128]{2,1,0:T(8,128)(2,1)}), bf16[128,72,128]{2,1,0:T(8,128)(2,1)S(1)}, u32[]{:S(2)}, u32[]{:S(2)}) async-start(bf16[128,72,128]{2,1,0:T(8,128)(2,1)} %copy-done.8), calls=%async_computation.1 | async-start | bytes 4718592 | tf_op jit(solution)/shard_map/all_to_all | solution.py:307
  95.0 1.3 copy-start.5
  96.3 1.3 copy-start.7
  97.6 0.9 copy-start.10
  98.5 0.8 copy-start.15
  99.2 0.7 copy-start.21
  110.7 2.9 %copy-start = (bf16[12,6,128,384]{3,2,1,0:T(8,128)(2,1)}, bf16[12,6,128,384]{3,2,1,0:T(8,128)(2,1)S(1)}, u32[]{:S(2)}) copy-start(bf16[12,6,128,384]{3,2,1,0:T(8,128)(2,1)S(1)} %get-tuple-element.7.saved_ref) | copy-start | bytes 21233668
  113.6 0.7 copy-start.12
  128.4 3.0 %copy-start.1 = (bf16[12,6,128,384]{3,2,1,0:T(8,128)(2,1)S(1)}, bf16[12,6,128,384]{3,2,1,0:T(8,128)(2,1)}, u32[]{:S(2)}) copy-start(bf16[12,6,128,384]{3,2,1,0:T(8,128)(2,1)} %copy-done) | copy-start | bytes 21233668
  131.4 0.9 copy-start.11
  132.4 0.9 copy-start.13
  (8 other events, 5.2 us)

commit v2 on v1

--- a/solution.py
+++ b/solution.py
@@ -62,7 +62,7 @@
         dst[pl.ds(pl.multiple_of(i * 192, 8), 192), :] = src[pl.ds(at, 8)].astype(F32).reshape(192, C)
         return 0
 
-    lax.fori_loop(0, ROWS // 8, body, 0)
+    lax.fori_loop(0, ROWS // 8, body, 0, unroll=2)
 
 
 def gather_cols(src, q):
@@ -79,7 +79,7 @@
 def row_code(mask_ref, chain_ref):
     half = lax.axis_index("half")
     code = jnp.where(mask_ref[...] > 0, chain_ref[...], -1)
-    code = jnp.broadcast_to(code, (8, RES))
+    code = jnp.broadcast_to(code.reshape(1, RES), (8, RES))
     code = pltpu.roll(code, lax.rem(RES - half * ROWS, RES), 1)[:1]
     low = code[:, C : C + C]
     return code[:, :C], jnp.where(low_lanes((1, C)), low, swap(low))
@@ -150,14 +150,14 @@
         put(LR_B + HALF_COLS + q, jnp.where(low, swap(tail_l), tail_r))
         return 0
 
-    lax.fori_loop(0, HALF_COLS, body, 0)
+    lax.fori_loop(0, HALF_COLS, body, 0, unroll=3)
 
     def flush(c, _):
         at = pl.multiple_of(c * OUT_ROWS, 8)
         out_ref[c] = stage[pl.ds(at, OUT_ROWS), :].astype(BF16)
         return 0
 
-    lax.fori_loop(0, C, flush, 0)
+    lax.fori_loop(0, C, flush, 0, unroll=4)
 
 
 def save_kernel(
@@ -192,7 +192,7 @@
         inv_ref[q] = jnp.broadcast_to(inv_z, (8, 3 * C))
         return 0
 
-    lax.fori_loop(0, HALF_COLS, body, 0)
+    lax.fori_loop(0, HALF_COLS, body, 0, unroll=3)
 
 
 def channel_kernel(in_ref, out_ref, g, left, right, back_l, back_r):
@@ -219,7 +219,7 @@
             ref[at, :] = jnp.concatenate([a, b], 0).astype(BF16)
         return 0
 
-    lax.fori_loop(0, 16, gather, 0)
+    lax.fori_loop(0, 16, gather, 0,unroll=2)
     spans = [(ROWS * h, C) for h in range(4)] + [(ROWS * h + C, 64) for h in range(4)]
     ordered = jnp.concatenate([g[at : at + size, :] for at, size in spans], 0)
     back_l[...] = dot(right[...], ordered)
@@ -235,7 +235,7 @@
             out_ref[w * 4 + h] = jnp.concatenate([back_l[at, lanes], back_r[at, lanes], mixed], 0).astype(BF16)
         return 0
 
-    lax.fori_loop(0, 32, give, 0)
+    lax.fori_loop(0, 32, give, 0, unroll=2)
 
 
 def back_kernel(in_ref, saved_ref, inv_ref, w_ref, in_gain, out_ref, rows, cols, stage):
@@ -246,7 +246,7 @@
         rows[pl.ds(at, BACK_ROWS), :] = in_ref[c].astype(F32)
         return 0
 
-    lax.fori_loop(0, C, fill, 0)
+    lax.fori_loop(0, C, fill, 0,unroll=4)
 
     def body(q, _):
         low = low_lanes((C, C))
@@ -278,7 +278,7 @@
         stage[pl.ds(base + q + HALF_COLS, 64, stride=COLS), :] = grad[2 * C + 64 :]
         return 0
 
-    lax.fori_loop(0, HALF_COLS, body, 0)
+    lax.fori_loop(0, HALF_COLS, body, 0, unroll=3)
 
     def flush(i, _):
         at = pl.multiple_of(i * 8, 8)
@@ -289,16 +289,20 @@
     lax.fori_loop(0, ROWS // 8, flush, 0)
 
 
-def call(kernel, outs, scratch, args, smem=(), flops=0, moved=0, limit=30):
-    vmem, scal = pl.BlockSpec(memory_space=pltpu.VMEM), pl.BlockSpec(memory_space=pltpu.SMEM)
-    single = not isinstance(outs, tuple)
+def call(kernel, outs, scratch, args, smem=(), flops=0, moved=0, limit=69206016):
+    scal = pl.BlockSpec(memory_space=pltpu.SMEM)
+
+    def whole(x):
+        return pl.BlockSpec(x.shape, lambda i: (0,) * len(x.shape))
+
     return pl.pallas_call(
         kernel,
         out_shape=outs,
-        in_specs=[scal if n in smem else vmem for n in range(len(args))],
-        out_specs=vmem if single else tuple(vmem for _ in outs),
+        grid=(1,),
+        in_specs=[scal if n in smem else whole(x) for n, x in enumerate(args)],
+        out_specs=jax.tree.map(whole, outs),
         scratch_shapes=scratch,
-        compiler_params=pltpu.CompilerParams(vmem_limit_bytes=limit << 20),
+        compiler_params=pltpu.CompilerParams(vmem_limit_bytes=limit),
         cost_estimate=pl.CostEstimate(flops=flops, bytes_accessed=moved, transcendentals=0),
     )(*args)
 
@@ -324,7 +328,7 @@
     shape = jax.ShapeDtypeStruct
     gains = [g.reshape(1, C) for g in (in_gain, in_bias, out_gain, out_bias)]
     given = [
-        pair_act, tri_out, cotangent, residue_mask.reshape(1, RES), chain_index.reshape(1, RES),
+        pair_act, tri_out, cotangent, residue_mask, chain_index,
         residue_mask, chain_index, chain_pairs, in_weight, out_weight, *gains,
     ]
     smem = (5, 6, 7)

time: 142 us -> 128 us (0.901)
  local copies, waits for them, and re-layouts: 29.5 us -> 0 us
  waiting for transfers between devices: 14.2 us -> 22.2 us
  Pallas kernels: 34.3 us -> 41.1 us
    unnamed x62 -> x0, local copies, waits for them, and re-layouts: 28.2 us -> none
    all_to_all x1, waiting for transfers between devices: 14.2 us -> 22.2 us  [exchange(): return lax.all_to_all(x, AXES, split_axis=0, concat_axis=0, tiled=True)]
    pallas_call x4, Pallas kernels: 34.3 us -> 41.1 us  [call(): pl.pallas_call(kernel, out_shape=outs, grid=(1,), in_specs=[scal if n in...]
  transfers between devices with their start and end apart: 1 -> 1, of which waited for: 1 -> 1; matrix products, arithmetic and copies ran while one was open for 0% -> 0% of each run, Pallas kernels for 6% -> 9%
where the time goes in v2:
time: 128 us
  blocking collectives  59.1 us (46%)
  Pallas kernels  41.1 us (32%)
  waiting for transfers between devices  22.2 us (17%)
  starting transfers between devices  5.5 us (4%)
    all_to_all x1, blocking collectives, exchange(): return lax.all_to_all(x, AXES, split_axis=0, concat_axis=0, tiled=True)  59.1 us
    pallas_call x4, Pallas kernels, call(): pl.pallas_call(kernel, out_shape=outs, grid=(1,), in_specs=[scal if n in...  41.1 us
    all_to_all x1, waiting for transfers between devices, exchange(): return lax.all_to_all(x, AXES, split_axis=0, concat_axis=0, tiled=True)  22.2 us
    all_to_all x1, starting transfers between devices, exchange(): return lax.all_to_all(x, AXES, split_axis=0, concat_axis=0, tiled=True)  5.5 us
  transfers between devices with their start and end apart: 1, of which 1 were waited for; matrix products, arithmetic and copies ran while one was open for 0% of the time, Pallas kernels for 9%

profile of v2, /device:TPU:1, one launch (start us, length us, event | category | flops | bytes accessed | tf_op | source)
XLA Modules:
  0.0 127.9 jit_solution(17631146758870760156)
XLA Ops:
  0.0 13.4 %shard_map.118 = bf16[128,112,128]{2,1,0:T(8,128)(2,1)} custom-call(bf16[192,24,128]{2,1,0:T(8,128)(2,1)} %pair_ref.3, bf16[192,24,128]{2,1,0:T(8,128)(2,1)} %tri_ref.3, bf16[192,24,128]{2,1,0:T(8,128)(2,1)} %cot_ref.3, s32[768]{0:T(1024)} %mask_s.3, s32[768]{0:T(1024)} %chain_s.3, s32[768]{0:T(1024)} %mask_s.3, s32[768]{0:T(1024)} %chain_s.3, ...), custom_call_target="tpu_custom_call" | custom-call | flops 905969664 | bytes 8388608 | tf_op jit(solution)/shard_map/pallas_call | solution.py:298
  13.4 59.1 %all_to_all.10.in_ref = bf16[128,112,128]{2,1,0:T(8,128)(2,1)} all-to-all(bf16[128,112,128]{2,1,0:T(8,128)(2,1)} %shard_map.118), channel_id=1, replica_groups=mesh['ch'=32,'half'=4] {'ch','half'}, dimensions={0} | all-to-all | bytes 7340032 | tf_op jit(solution)/shard_map/all_to_all | solution.py:311
  72.5 7.9 %shard_map.119 = bf16[128,72,128]{2,1,0:T(8,128)(2,1)} custom-call(bf16[128,112,128]{2,1,0:T(8,128)(2,1)} %all_to_all.10.in_ref), custom_call_target="tpu_custom_call" | custom-call | flops 1811939328 | bytes 8388608 | tf_op jit(solution)/shard_map/pallas_call | solution.py:298
  80.4 5.5 %all-to-all-start.1 = ((bf16[128,72,128]{2,1,0:T(8,128)(2,1)}), bf16[128,72,128]{2,1,0:T(8,128)(2,1)}, u32[]{:S(2)}, u32[]{:S(2)}) async-start(bf16[128,72,128]{2,1,0:T(8,128)(2,1)} %shard_map.119), calls=%async_computation.1 | async-start | bytes 4718592 | tf_op jit(solution)/shard_map/all_to_all | solution.py:311
  85.9 10.9 %shard_map.120 = (bf16[12,6,128,384]{3,2,1,0:T(8,128)(2,1)}, f32[12,8,384]{2,1,0:T(8,128)}) custom-call(bf16[192,24,128]{2,1,0:T(8,128)(2,1)} %pair_ref.3, bf16[192,24,128]{2,1,0:T(8,128)(2,1)} %tri_ref.3, bf16[192,24,128]{2,1,0:T(8,128)(2,1)} %cot_ref.3, s32[768]{0:T(1024)} %mask_s.3, s32[768]{0:T(1024)} %chain_s.3, s32[768]{0:T(1024)} %mask_s.3, ...), custom_call_target="tpu_custom_call" | custom-call | flops 905969664 | bytes 12582912 | tf_op jit(solution)/shard_map/pallas_call | solution.py:298
  96.9 22.2 %all-to-all-done.1.in_ref = bf16[128,72,128]{2,1,0:T(8,128)(2,1)} async-done(((bf16[128,72,128]{2,1,0:T(8,128)(2,1)}), bf16[128,72,128]{2,1,0:T(8,128)(2,1)}, u32[]{:S(2)}, u32[]{:S(2)}) %all-to-all-start.1) | async-done | bytes 2359328 | tf_op jit(solution)/shard_map/all_to_all | solution.py:311
  119.1 8.8 %shard_map.121 = bf16[192,24,128]{2,1,0:T(8,128)(2,1)} custom-call(bf16[128,72,128]{2,1,0:T(8,128)(2,1)} %all-to-all-done.1.in_ref, bf16[12,6,128,384]{3,2,1,0:T(8,128)(2,1)} %get-tuple-element.7.saved_ref, f32[12,8,384]{2,1,0:T(8,128)} %get-tuple-element.8.inv_ref, bf16[128,640]{1,0:T(8,128)(2,1)} %w_ref.5, f32[1,128]{1,0:T(1,128)} %bitcast.6), custom_call_target="tpu_custom_call" | custom-call | flops 754974720 | bytes 12582912 | tf_op jit(solution)/shard_map/pallas_call | solution.py:298
Async XLA Ops:
  80.4 38.7 %all-to-all-start.1 = ((bf16[128,72,128]{2,1,0:T(8,128)(2,1)}), bf16[128,72,128]{2,1,0:T(8,128)(2,1)}, u32[]{:S(2)}, u32[]{:S(2)}) async-start(bf16[128,72,128]{2,1,0:T(8,128)(2,1)} %shard_map.119), calls=%async_computation.1 | async-start | bytes 4718592 | tf_op jit(solution)/shard_map/all_to_all | solution.py:311

commit v3 on v2

v3 whole, which is shorter than its diff:
```python
import jax
import jax.numpy as jnp
from jax import lax
from jax.experimental import pallas as pl
from jax.experimental.pallas import tpu as pltpu
from jax.sharding import PartitionSpec as P

EPSILON = 1e-05
AXES = ("ch", "half")
F32 = jnp.float32
BF16 = jnp.bfloat16

ROWS, COLS, C, RES = 192, 24, 128, 768
GROUP, PAIRS, GROUPS = 8, 4, 3
STEP, TAIL_AT, TAIL, OUT_ROWS = 32, 96, 16, 112
BACK_STEP, BACK_ROWS = 24, 72
X_PITCH, OUT_PITCH, TAIL_PITCH, BACK_PITCH = 9, 33, 17, 25
SPAN = 8


def dot(a, b):
    return jnp.dot(a, b, preferred_element_type=F32)


def mean(x):
    return jnp.sum(x, 0, keepdims=True) * (1.0 / C)


def centre(x):
    centred = x - mean(x)
    return centred, lax.rsqrt(mean(centred * centred) + EPSILON)


def column(row):
    return jnp.broadcast_to(row, (C, C)).T


def swap(x):
    return pltpu.roll(x, 64, 1)


def low_lanes(shape):
    return lax.broadcasted_iota(jnp.int32, shape, 1) < 64


def spread(src, dst):
    def body(i, _):
        values = src[pl.ds(pl.multiple_of(i * 16, 16), 16)].astype(F32)
        for n in range(16):
            dst[pl.ds((i * 16 + n) * X_PITCH, GROUP), :] = values[n]
        return 0

    lax.fori_loop(0, ROWS // 16, body, 0, unroll=2)


def gather(src, q, part):
    if part < 2:
        return src[pl.ds(q + PAIRS * part, C, stride=X_PITCH), :].T
    base = C * X_PITCH
    tails = [src[pl.ds(base + q + PAIRS * n, 64, stride=X_PITCH), :] for n in range(2)]
    return jnp.concatenate(tails, 0).T


def row_code(mask_ref, chain_ref):
    half = lax.axis_index("half")
    code = jnp.where(mask_ref[...] > 0, chain_ref[...], -1)
    code = jnp.broadcast_to(code.reshape(1, RES), (8, RES))
    code = pltpu.roll(code, lax.rem(RES - half * ROWS, RES), 1)[:1]
    tail = code[:, C : C + C]
    return code[:, :C], jnp.where(low_lanes((1, C)), tail, swap(tail))


def keep_rows(q, codes, mask_s, chain_s, pairs_s):
    first = lax.axis_index("ch") * COLS + q

    def pick(code, k):
        chain, out = chain_s[k], jnp.zeros(code.shape, F32)
        for c in range(4):
            out = jnp.where(code == c, 0.5 * (pairs_s[c, chain] * mask_s[k]).astype(F32), out)
        return out

    code_a, code_b = codes
    tail = jnp.where(low_lanes((1, C)), pick(code_b, first), pick(code_b, first + PAIRS))
    return pick(code_a, first), pick(code_a, first + PAIRS), tail


def prepare(w_ref, wo_ref, gains, wt, wot, cols):
    for n in range(5):
        part = w_ref[:, n * C : (n + 1) * C].astype(F32).T
        wt[n] = (part * 0.5 if n in (1, 3, 4) else part).astype(BF16)
    wot[...] = wo_ref[...].astype(F32).T.astype(BF16)
    for n, g in enumerate(gains):
        cols[n] = column(g[...])
    cols[4] = cols[2] * 0.5


def front_kernel(
    pair_ref, tri_ref, cot_ref, mask_v, chain_v, mask_s, chain_s, pairs_s,
    w_ref, wo_ref, in_gain, in_bias, out_gain, out_bias, out_ref,
    xp, xt, xc, wt, wot, cols, stage, stage_tail, packed, sems,
):
    group = pl.program_id(0)

    @pl.when(group == 0)
    def _():
        prepare(w_ref, wo_ref, (in_gain, in_bias, out_gain, out_bias), wt, wot, cols)
        for r in range(4):
            stage_tail[pl.ds(12 + r, C, stride=TAIL_PITCH), :] = jnp.zeros((C, C), F32)

    spread(pair_ref, xp)
    spread(tri_ref, xt)
    spread(cot_ref, xc)
    codes = row_code(mask_v, chain_v)

    def put(row, value):
        stage[pl.ds(row, C, stride=OUT_PITCH), :] = value

    def body(q, _):
        keeps = keep_rows(group * GROUP + q, codes, mask_s, chain_s, pairs_s)
        for part in range(3):
            centred, inv = centre(gather(xp, q, part))
            nz = (centred * inv * cols[0] + cols[1]).astype(BF16)
            keep = keeps[part]
            left = (jnp.tanh(dot(wt[1], nz)) + 1.0) * (dot(wt[0], nz) * keep)
            right = (jnp.tanh(dot(wt[3], nz)) + 1.0) * (dot(wt[2], nz) * keep)
            outer = ((jnp.tanh(dot(wt[4], nz)) + 1.0) * gather(xc, q, part)).astype(BF16)
            centred, inv = centre(gather(xt, q, part))
            h = dot(wo_ref[...], outer) * cols[4]
            second = mean(h * centred) * (inv * inv)
            grad = inv * (h - mean(h) - centred * second)
            if part < 2:
                put(q + PAIRS * part, grad)
                put(GROUP + q + PAIRS * part, left)
                put(2 * GROUP + q + PAIRS * part, right)
            else:
                low = low_lanes((C, C))
                stage_tail[pl.ds(group * PAIRS + q, C, stride=TAIL_PITCH), :] = grad
                put(3 * GROUP + q, jnp.where(low, left, swap(right)))
                put(3 * GROUP + PAIRS + q, jnp.where(low, swap(left), right))
        return 0

    lax.fori_loop(0, PAIRS, body, 0, unroll=4)

    def send(n):
        rows = pl.ds(n * STEP, STEP)
        return pltpu.make_async_copy(packed.at[:, rows], out_ref.at[:, rows], sems.at[n])

    tail = pl.ds(TAIL_AT, TAIL)
    send_tail = pltpu.make_async_copy(packed.at[:, tail], out_ref.at[:, tail], sems.at[GROUPS])
    for n in range(GROUPS):

        @pl.when(group == n)
        def _(n=n):
            def flush(c, _):
                packed[c, n * STEP : (n + 1) * STEP] = stage[pl.ds(c * OUT_PITCH, STEP), :].astype(BF16)
                return 0

            lax.fori_loop(0, C, flush, 0, unroll=8)
            send(n).start()

    @pl.when(group == GROUPS - 1)
    def _():
        def flush(c, _):
            packed[c, TAIL_AT:] = stage_tail[pl.ds(c * TAIL_PITCH, TAIL), :].astype(BF16)
            return 0

        lax.fori_loop(0, C, flush, 0, unroll=8)
        send_tail.start()
        for n in range(GROUPS):
            send(n).wait()
        send_tail.wait()


def save_kernel(
    pair_ref, tri_ref, cot_ref, mask_v, chain_v, mask_s, chain_s, pairs_s,
    w_ref, wo_ref, in_gain, in_bias, out_gain, out_bias, saved_ref, inv_ref,
    xp, xt, xc, wt, wot, cols,
):
    group = pl.program_id(0)

    @pl.when(group == 0)
    def _():
        prepare(w_ref, wo_ref, (in_gain, in_bias, out_gain, out_bias), wt, wot, cols)

    spread(pair_ref, xp)
    spread(tri_ref, xt)
    spread(cot_ref, xc)
    codes = row_code(mask_v, chain_v)

    def body(q, _):
        keeps = keep_rows(group * GROUP + q, codes, mask_s, chain_s, pairs_s)
        for part in range(3):
            centred, inv = centre(gather(xp, q, part))
            unit_z = centred * inv
            nz = (unit_z * cols[0] + cols[1]).astype(BF16)
            keep = keeps[part]
            for n in (0, 1):
                gate = jnp.tanh(dot(wt[2 * n + 1], nz))
                kept = (gate + 1.0) * keep
                saved_ref[q, part, 2 * n] = kept.astype(BF16)
                saved_ref[q, part, 2 * n + 1] = (kept * dot(wt[2 * n], nz) * (0.5 - 0.5 * gate)).astype(BF16)
            gate = jnp.tanh(dot(wt[4], nz))
            centred, inv_x = centre(gather(xt, q, part))
            nx = (centred * inv_x * cols[2] + cols[3]).astype(BF16)
            slope = (0.5 + 0.5 * gate) * (0.5 - 0.5 * gate)
            saved_ref[q, part, 4] = (gather(xc, q, part) * dot(wot[...], nx) * slope).astype(BF16)
            saved_ref[q, part, 5] = unit_z.astype(BF16)
            inv_ref[q, part] = jnp.broadcast_to(inv, (8, C))
        return 0

    lax.fori_loop(0, PAIRS, body, 0)


def channel_kernel(in_ref, out_ref, g, left, right, ordered):
    step = pl.program_id(0)
    steps = 32 // SPAN
    low8, low16 = low_lanes((GROUP, C)), low_lanes((TAIL, C))

    def take(w):
        blocks = [in_ref[w * 4 + h].astype(F32) for h in range(4)]

        def part(n):
            return [jnp.concatenate([b[STEP * m + GROUP * n : STEP * m + GROUP * (n + 1)] for m in range(3)], 0) for b in blocks]

        rows_g, rows_l, rows_r, mixed = part(0), part(1), part(2), part(3)
        low24 = low_lanes((COLS, C))
        for h in (0, 2):
            a, b = blocks[h][TAIL_AT:], blocks[h + 1][TAIL_AT:]
            one, two = jnp.where(low16, a, swap(b)), jnp.where(low16, swap(a), b)
            pieces = [x[PAIRS * m : PAIRS * (m + 1)] for m in range(3) for x in (one, two)]
            rows_g.append(jnp.concatenate(pieces, 0))
            a, b = mixed[h], mixed[h + 1]
            rows_l.append(jnp.where(low24, a, swap(b)))
            rows_r.append(jnp.where(low24, swap(a), b))
        return [jnp.concatenate(rows, 1) for rows in (rows_g, rows_l, rows_r)]

    @pl.when(step < steps)
    def _():
        def body(pair, _):
            one, two = take(2 * pair), take(2 * pair + 1)
            at = pl.ds(pl.multiple_of(step * (SPAN * COLS) + pair * 48, 16), 48)
            for ref, a, b in zip((g, left, right), one, two):
                ref[at, :] = jnp.concatenate([a, b], 0).astype(BF16)
            return 0

        lax.fori_loop(0, SPAN // 2, body, 0, unroll=2)

    @pl.when(step == steps)
    def _():
        to = 0
        for at, size in [(ROWS * h, C) for h in range(4)] + [(ROWS * h + C, 64) for h in range(4)]:
            ordered[to : to + size] = g[at : at + size]
            to += size

    @pl.when(step >= steps)
    def _():
        rows = pl.ds(pl.multiple_of((step - steps) * (SPAN * COLS), SPAN * COLS), SPAN * COLS)
        back_l = dot(right[rows, :], ordered[...])
        back_r = lax.dot_general(left[rows, :], ordered[...], (((1,), (1,)), ((), ())), preferred_element_type=F32)
        for w in range(SPAN):
            for h in range(4):
                lanes, tail = slice(h * C, (h + 1) * C), slice((4 + h // 2) * C, (5 + h // 2) * C)
                pieces = []
                for m in range(3):
                    at = slice(w * COLS + m * GROUP, w * COLS + (m + 1) * GROUP)
                    a, b = back_l[at, tail], back_r[at, tail]
                    mixed = jnp.where(low8, a, swap(b)) if h % 2 == 0 else jnp.where(low8, swap(a), b)
                    pieces += [back_l[at, lanes], back_r[at, lanes], mixed]
                out_ref[w * 4 + h] = jnp.concatenate(pieces, 0).astype(BF16)


def back_kernel(in_ref, saved_ref, inv_ref, w_ref, in_gain, out_ref, rows, cols, stage):
    group = pl.program_id(0)

    @pl.when(group == 0)
    def _():
        cols[...] = column(in_gain[...])

    def fill(c, _):
        rows[pl.ds(c * BACK_PITCH, BACK_STEP), :] = in_ref[c].astype(F32)
        return 0

    lax.fori_loop(0, C, fill, 0, unroll=8)

    def body(q, _):
        low = low_lanes((C, C))

        def get(row):
            return rows[pl.ds(row, C, stride=BACK_PITCH), :]

        a, b = get(2 * GROUP + q), get(2 * GROUP + PAIRS + q)
        lefts = [get(q), get(PAIRS + q), jnp.where(low, a, swap(b))]
        rights = [get(GROUP + q), get(GROUP + PAIRS + q), jnp.where(low, swap(a), b)]
        for part in range(3):
            saved = saved_ref.at[q, part]
            grad_l, grad_r = lefts[part].astype(BF16), rights[part].astype(BF16)
            pieces = [grad_l * saved[0], grad_l * saved[1], grad_r * saved[2], grad_r * saved[3], saved[4]]
            e = dot(w_ref[...], jnp.concatenate(pieces, 0)) * cols[...]
            unit_z = saved[5].astype(F32)
            grad = (inv_ref[q, part][:1] * (e - mean(e) - unit_z * mean(e * unit_z))).T
            if part < 2:
                stage[pl.ds(q + PAIRS * part, C, stride=X_PITCH), :] = grad
            else:
                base = C * X_PITCH
                stage[pl.ds(base + q, 64, stride=X_PITCH), :] = grad[:64]
                stage[pl.ds(base + q + PAIRS, 64, stride=X_PITCH), :] = grad[64:]
        return 0

    lax.fori_loop(0, PAIRS, body, 0, unroll=4)

    def flush(i, _):
        at = pl.multiple_of(i * 16, 16)
        rows16 = [stage[pl.ds((i * 16 + n) * X_PITCH, GROUP), :].reshape(1, GROUP, C) for n in range(16)]
        out_ref[pl.ds(at, 16)] = jnp.concatenate(rows16, 0).astype(BF16)
        return 0

    lax.fori_loop(0, ROWS // 16, flush, 0, unroll=2)


def whole(x):
    return pl.BlockSpec(x.shape, lambda i: (0,) * len(x.shape))


def call(kernel, grid, ins, outs, out_specs, scratch, args, flops, moved):
    return pl.pallas_call(
        kernel,
        out_shape=outs,
        grid=(grid,),
        in_specs=ins,
        out_specs=out_specs,
        scratch_shapes=scratch,
        compiler_params=pltpu.CompilerParams(vmem_limit_bytes=66 << 20),
        cost_estimate=pl.CostEstimate(flops=flops, bytes_accessed=moved, transcendentals=0),
    )(*args)


def exchange(x):
    return lax.all_to_all(x, AXES, split_axis=0, concat_axis=0, tiled=True)


def on_device(
    pair_act,
    tri_out,
    cotangent,
    residue_mask,
    chain_index,
    chain_pairs,
    in_weight,
    out_weight,
    in_gain,
    in_bias,
    out_gain,
    out_bias,
):
    shape = jax.ShapeDtypeStruct
    gains = [g.reshape(1, C) for g in (in_gain, in_bias, out_gain, out_bias)]
    given = [
        pair_act, tri_out, cotangent, residue_mask, chain_index,
        residue_mask, chain_index, chain_pairs, in_weight, out_weight, *gains,
    ]
    scalars = pl.BlockSpec(memory_space=pltpu.SMEM)
    tile = pl.BlockSpec((ROWS, GROUP, C), lambda i: (0, i, 0))
    given_specs = [tile] * 3 + [whole(x) for x in given[3:5]] + [scalars] * 3 + [whole(x) for x in given[8:]]
    part = pltpu.VMEM((ROWS * X_PITCH, C), F32)
    shared = [part, part, part, pltpu.VMEM((5, C, C), BF16), pltpu.VMEM((C, C), BF16), pltpu.VMEM((5, C, C), F32)]
    sent = call(
        front_kernel,
        GROUPS,
        given_specs,
        shape((C, OUT_ROWS, C), BF16),
        pl.BlockSpec(memory_space=pl.ANY),
        shared
        + [
            pltpu.VMEM((C * OUT_PITCH, C), F32),
            pltpu.VMEM((C * TAIL_PITCH, C), F32),
            pltpu.VMEM((C, OUT_ROWS, C), BF16),
            pltpu.SemaphoreType.DMA((GROUPS + 1,)),
        ],
        given,
        2 * 4608 * 128 * 768,
        8 << 20,
    )
    saved, inv = call(
        save_kernel,
        GROUPS,
        given_specs,
        (shape((GROUPS * PAIRS, 3, 6, C, C), BF16), shape((GROUPS * PAIRS, 3, 8, C), F32)),
        (
            pl.BlockSpec((PAIRS, 3, 6, C, C), lambda i: (i, 0, 0, 0, 0)),
            pl.BlockSpec((PAIRS, 3, 8, C), lambda i: (i, 0, 0, 0)),
        ),
        shared,
        given,
        2 * 4608 * 128 * 768,
        12 << 20,
    )
    got = exchange(sent)
    square = pltpu.VMEM((RES, RES), BF16)
    steps = 32 // SPAN
    back = call(
        channel_kernel,
        2 * steps,
        [pl.BlockSpec((4 * SPAN, OUT_ROWS, C), lambda i: (jnp.minimum(i, steps - 1), 0, 0))],
        shape((C, BACK_ROWS, C), BF16),
        pl.BlockSpec((4 * SPAN, BACK_ROWS, C), lambda i: (jnp.maximum(i - steps, 0), 0, 0)),
        [square, square, square, square],
        [got],
        4 * RES**3,
        8 << 20,
    )
    returned = exchange(back)
    return call(
        back_kernel,
        GROUPS,
        [
            pl.BlockSpec((C, BACK_STEP, C), lambda i: (0, i, 0)),
            pl.BlockSpec((PAIRS, 3, 6, C, C), lambda i: (i, 0, 0, 0, 0)),
            pl.BlockSpec((PAIRS, 3, 8, C), lambda i: (i, 0, 0, 0)),
            whole(in_weight),
            whole(gains[0]),
        ],
        shape((ROWS, COLS, C), BF16),
        tile,
        [pltpu.VMEM((C * BACK_PITCH, C), F32), pltpu.VMEM((C, C), F32), part],
        [returned, saved, inv, in_weight, gains[0]],
        2 * 4608 * 128 * 640,
        12 << 20,
    )


def solution(mesh):
    return jax.shard_map(
        on_device,
        mesh=mesh,
        in_specs=(P("half", "ch", None),) * 3 + (P(),) * 9,
        out_specs=P("half", "ch", None),
        check_vma=False,
    )
```

time: 128 us -> 121 us (0.945)
  Pallas kernels: 41.1 us -> 33.4 us
    pallas_call x4, Pallas kernels: 41.1 us -> 33.4 us  [call(): pl.pallas_call(kernel, out_shape=outs, grid=(grid,), in_specs=ins, out_sp...]
  transfers between devices with their start and end apart: 1 -> 1, of which waited for: 1 -> 1; matrix products, arithmetic and copies ran while one was open for 0% -> 0% of each run, Pallas kernels for 9% -> 8%
where the time goes in v3:
time: 121 us
  blocking collectives  59.1 us (49%)
  Pallas kernels  33.4 us (28%)
  waiting for transfers between devices  23 us (19%)
  starting transfers between devices  5.5 us (5%)
    all_to_all x1, blocking collectives, exchange(): return lax.all_to_all(x, AXES, split_axis=0, concat_axis=0, tiled=True)  59.1 us
    pallas_call x4, Pallas kernels, call(): pl.pallas_call(kernel, out_shape=outs, grid=(grid,), in_specs=ins, out_sp...  33.4 us
    all_to_all x1, waiting for transfers between devices, exchange(): return lax.all_to_all(x, AXES, split_axis=0, concat_axis=0, tiled=True)  23 us
    all_to_all x1, starting transfers between devices, exchange(): return lax.all_to_all(x, AXES, split_axis=0, concat_axis=0, tiled=True)  5.5 us
  transfers between devices with their start and end apart: 1, of which 1 were waited for; matrix products, arithmetic and copies ran while one was open for 0% of the time, Pallas kernels for 8%

profile of v3, /device:TPU:1, one launch (start us, length us, event | category | flops | bytes accessed | tf_op | source)
XLA Modules:
  0.0 121.1 jit_solution(9354108029368997482)
XLA Ops:
  0.0 8.5 %shard_map.118 = bf16[128,112,128]{2,1,0:T(8,128)(2,1)} custom-call(bf16[192,24,128]{2,1,0:T(8,128)(2,1)} %pair_ref.3, bf16[192,24,128]{2,1,0:T(8,128)(2,1)} %tri_ref.3, bf16[192,24,128]{2,1,0:T(8,128)(2,1)} %cot_ref.3, s32[768]{0:T(1024)} %mask_s.3, s32[768]{0:T(1024)} %chain_s.3, s32[768]{0:T(1024)} %mask_s.3, s32[768]{0:T(1024)} %chain_s.3, ...), custom_call_target="tpu_custom_call" | custom-call | flops 905969664 | bytes 8388608 | tf_op jit(solution)/shard_map/pallas_call | solution.py:325
  8.5 59.1 %all_to_all.10.in_ref = bf16[128,112,128]{2,1,0:T(8,128)(2,1)} all-to-all(bf16[128,112,128]{2,1,0:T(8,128)(2,1)} %shard_map.118), channel_id=1, replica_groups=mesh['ch'=32,'half'=4] {'ch','half'}, dimensions={0} | all-to-all | bytes 7340032 | tf_op jit(solution)/shard_map/all_to_all | solution.py:338
  67.6 7.8 %shard_map.119 = bf16[128,72,128]{2,1,0:T(8,128)(2,1)} custom-call(bf16[128,112,128]{2,1,0:T(8,128)(2,1)} %all_to_all.10.in_ref), custom_call_target="tpu_custom_call" | custom-call | flops 1811939328 | bytes 8388608 | tf_op jit(solution)/shard_map/pallas_call | solution.py:325
  75.5 5.5 %all-to-all-start.1 = ((bf16[128,72,128]{2,1,0:T(8,128)(2,1)}), bf16[128,72,128]{2,1,0:T(8,128)(2,1)}, u32[]{:S(2)}, u32[]{:S(2)}) async-start(bf16[128,72,128]{2,1,0:T(8,128)(2,1)} %shard_map.119), calls=%async_computation.1 | async-start | bytes 4718592 | tf_op jit(solution)/shard_map/all_to_all | solution.py:338
  81.0 10.2 %shard_map.120 = (bf16[12,3,6,128,128]{4,3,2,1,0:T(8,128)(2,1)}, f32[12,3,8,128]{3,2,1,0:T(8,128)}) custom-call(bf16[192,24,128]{2,1,0:T(8,128)(2,1)} %pair_ref.3, bf16[192,24,128]{2,1,0:T(8,128)(2,1)} %tri_ref.3, bf16[192,24,128]{2,1,0:T(8,128)(2,1)} %cot_ref.3, s32[768]{0:T(1024)} %mask_s.3, s32[768]{0:T(1024)} %chain_s.3, s32[768]{0:T(1024)} %mask_s.3, ...), custom_call_target="tpu_custom_call" | custom-call | flops 905969664 | bytes 12582912 | tf_op jit(solution)/shard_map/pallas_call | solution.py:325
  91.1 23.0 %all-to-all-done.1.in_ref = bf16[128,72,128]{2,1,0:T(8,128)(2,1)} async-done(((bf16[128,72,128]{2,1,0:T(8,128)(2,1)}), bf16[128,72,128]{2,1,0:T(8,128)(2,1)}, u32[]{:S(2)}, u32[]{:S(2)}) %all-to-all-start.1) | async-done | bytes 2359328 | tf_op jit(solution)/shard_map/all_to_all | solution.py:338
  114.1 6.9 %shard_map.121 = bf16[192,24,128]{2,1,0:T(8,128)(2,1)} custom-call(bf16[128,72,128]{2,1,0:T(8,128)(2,1)} %all-to-all-done.1.in_ref, bf16[12,3,6,128,128]{4,3,2,1,0:T(8,128)(2,1)} %get-tuple-element.7.saved_ref, f32[12,3,8,128]{3,2,1,0:T(8,128)} %get-tuple-element.8.inv_ref, bf16[128,640]{1,0:T(8,128)(2,1)} %w_ref.5, f32[1,128]{1,0:T(1,128)} %bitcast.6), custom_call_target="tpu_custom_call" | custom-call | flops 754974720 | bytes 12582912 | tf_op jit(solution)/shard_map/pallas_call | solution.py:325
Async XLA Ops:
  75.5 38.7 %all-to-all-start.1 = ((bf16[128,72,128]{2,1,0:T(8,128)(2,1)}), bf16[128,72,128]{2,1,0:T(8,128)(2,1)}, u32[]{:S(2)}, u32[]{:S(2)}) async-start(bf16[128,72,128]{2,1,0:T(8,128)(2,1)} %shard_map.119), calls=%async_computation.1 | async-start | bytes 4718592 | tf_op jit(solution)/shard_map/all_to_all | solution.py:338

commit v4 on v0

v4 whole, which is shorter than its diff:
```python
import jax
import jax.numpy as jnp
from jax import lax
from jax.experimental import pallas as pl
from jax.experimental.pallas import tpu as pltpu
from jax.sharding import PartitionSpec as P

EPSILON = 1e-05
AXES = ("ch", "half")
F32 = jnp.float32
BF16 = jnp.bfloat16

ROWS, COLS, C, RES = 192, 24, 128, 768
GROUP, PAIRS, GROUPS = 8, 4, 3
STEP, TAIL_AT, TAIL, OUT_ROWS = 32, 96, 16, 112
BACK_STEP, BACK_ROWS = 24, 72
X_PITCH, OUT_PITCH, TAIL_PITCH, BACK_PITCH = GROUP + 1, STEP + 1, TAIL + 1, BACK_STEP + 1
X_SIZE, OUT_SIZE, BACK_SIZE = ROWS * X_PITCH, C * OUT_PITCH, C * BACK_PITCH
FETCHES = 8
CHUNKS = 4
CHUNK = RES // CHUNKS


def dot(a, b):
    return jnp.dot(a, b, preferred_element_type=F32)


def mean(x):
    return jnp.sum(x, 0, keepdims=True) * (1.0 / C)


def centre(x):
    centred = x - mean(x)
    return centred, lax.rsqrt(mean(centred * centred) + EPSILON)


def column(row):
    return jnp.broadcast_to(row[...].reshape(1, C), (C, C)).T


def swap(x):
    return pltpu.roll(x, 64, 1)


def low_lanes(shape):
    return lax.broadcasted_iota(jnp.int32, shape, 1) < 64


def copies(sources, targets, sems):
    started = [pltpu.make_async_copy(s, t, sems.at[n]) for n, (s, t) in enumerate(zip(sources, targets))]
    for copy in started:
        copy.start()
    return started


def spread(tiles, x, group):
    for n in range(3):

        def body(i, _):
            values = tiles[group, n, pl.ds(pl.multiple_of(i * 16, 16), 16)].astype(F32)
            for m in range(16):
                x[n, pl.ds((i * 16 + m) * X_PITCH, GROUP), :] = values[m]
            return 0

        lax.fori_loop(0, ROWS // 16, body, 0, unroll=2)


def gather(x, n, q, part):
    if part < 2:
        return x[n, pl.ds(q + PAIRS * part, C, stride=X_PITCH), :].T
    base = C * X_PITCH + q
    return jnp.concatenate([x[n, pl.ds(base + PAIRS * m, 64, stride=X_PITCH), :] for m in range(2)], 0).T


def find_keep(mask_v, chain_v, pairs_v, keep):
    code = jnp.where(mask_v[...] > 0, chain_v[...], -1)
    code = jnp.broadcast_to(code.reshape(1, RES), (8, RES))
    rows = pltpu.roll(code, lax.rem(RES - lax.axis_index("half") * ROWS, RES), 1)[:1]
    cols = pltpu.roll(code, lax.rem(RES - lax.axis_index("ch") * COLS, RES), 1)[:1, :C]
    cols = jnp.broadcast_to(cols, (C, C)).astype(F32).T[:COLS]
    tail = rows[:, C : 2 * C]
    tail = jnp.where(low_lanes((1, C)), tail, swap(tail))
    pairs = pairs_v[...].astype(F32) * 0.5
    for n, rows_n in enumerate((rows[:, :C], tail)):
        out = jnp.zeros((COLS, C), F32)
        for d in range(4):
            across = jnp.zeros((1, C), F32)
            for c in range(4):
                across = jnp.where(rows_n == c, jnp.broadcast_to(pairs[c : c + 1, d : d + 1], (1, C)), across)
            out = jnp.where(cols == float(d), jnp.broadcast_to(across, (COLS, C)), out)
        keep[n] = out


def keep_of(keep, col, part):
    if part < 2:
        return keep[0, pl.ds(col + PAIRS * part, 1), :]
    return jnp.where(low_lanes((1, C)), keep[1, pl.ds(col, 1), :], keep[1, pl.ds(col + PAIRS, 1), :])


def prepare(given, buffers, wt, wot, cols, keep, sems):
    mask_v, chain_v, pairs_v, w_v, wo_v, *gains, tiles = buffers
    started = copies(given[3:], buffers[:-1], sems)

    def tile(group, n):
        at = pl.ds(pl.multiple_of(group * GROUP, GROUP), GROUP)
        return pltpu.make_async_copy(given[n].at[:, at], tiles.at[group, n], sems.at[9 + group * 3 + n])

    for group in range(GROUPS):
        for n in range(3):
            tile(group, n).start()
    for copy in started:
        copy.wait()
    for n in range(5):
        part = w_v[:, n * C : (n + 1) * C].astype(F32).T
        wt[n] = (part * 0.5 if n in (1, 3, 4) else part).astype(BF16)
    wot[...] = wo_v[...].astype(F32).T.astype(BF16)
    for n, g in enumerate(gains):
        cols[n] = column(g)
    cols[4] = cols[2] * 0.5
    find_keep(mask_v, chain_v, pairs_v, keep)

    def wait(group):
        for n in range(3):
            tile(group, n).wait()

    return wait


def front_kernel(*refs):
    given, out_ref = refs[:12], refs[12]
    *buffers, x, wt, wot, cols, keep, stage, stage_tail, packed, sems, out_sems = refs[13:]
    wo_v, tiles = buffers[4], buffers[-1]
    wait = prepare(given, buffers, wt, wot, cols, keep, sems)
    for r in range(4):
        stage_tail[pl.ds(12 + r, C, stride=TAIL_PITCH), :] = jnp.zeros((C, C), F32)

    def send(group):
        rows = pl.ds(pl.multiple_of(group * STEP, STEP), STEP)
        return pltpu.make_async_copy(packed.at[:, rows], out_ref.at[:, rows], out_sems.at[group])

    def body(group, _):
        wait(group)
        spread(tiles, x, group)
        for q in range(PAIRS):
            col = group * GROUP + q

            def put(row, value):
                stage[pl.ds(row, C, stride=OUT_PITCH), :] = value

            for part in range(3):
                centred, inv = centre(gather(x, 0, q, part))
                nz = (centred * inv * cols[0] + cols[1]).astype(BF16)
                kept = keep_of(keep, col, part)
                left = (jnp.tanh(dot(wt[1], nz)) + 1.0) * (dot(wt[0], nz) * kept)
                right = (jnp.tanh(dot(wt[3], nz)) + 1.0) * (dot(wt[2], nz) * kept)
                outer = ((jnp.tanh(dot(wt[4], nz)) + 1.0) * gather(x, 2, q, part)).astype(BF16)
                centred, inv = centre(gather(x, 1, q, part))
                h = dot(wo_v[...], outer) * cols[4]
                second = mean(h * centred) * (inv * inv)
                grad = inv * (h - mean(h) - centred * second)
                if part < 2:
                    put(q + PAIRS * part, grad)
                    put(GROUP + q + PAIRS * part, left)
                    put(2 * GROUP + q + PAIRS * part, right)
                else:
                    low = low_lanes((C, C))
                    stage_tail[pl.ds(group * PAIRS + q, C, stride=TAIL_PITCH), :] = grad
                    put(3 * GROUP + q, jnp.where(low, left, swap(right)))
                    put(3 * GROUP + PAIRS + q, jnp.where(low, swap(left), right))

        def pack(c, _):
            rows = pl.ds(pl.multiple_of(group * STEP, STEP), STEP)
            packed[c, rows] = stage[pl.ds(c * OUT_PITCH, STEP), :].astype(BF16)
            return 0

        lax.fori_loop(0, C, pack, 0, unroll=8)

        @pl.when(group < GROUPS - 1)
        def _():
            send(group).start()

        return 0

    lax.fori_loop(0, GROUPS, body, 0)

    def pack(c, _):
        packed[c, TAIL_AT:] = stage_tail[pl.ds(c * TAIL_PITCH, TAIL), :].astype(BF16)
        return 0

    lax.fori_loop(0, C, pack, 0, unroll=8)
    rest = pl.ds((GROUPS - 1) * STEP, OUT_ROWS - (GROUPS - 1) * STEP)
    final = pltpu.make_async_copy(packed.at[:, rest], out_ref.at[:, rest], out_sems.at[GROUPS - 1])
    final.start()
    for group in range(GROUPS - 1):
        send(group).wait()
    final.wait()


def save_kernel(*refs):
    given, saved_ref, inv_ref = refs[:12], refs[12], refs[13]
    *buffers, x, wt, wot, cols, keep, sems = refs[14:]
    tiles = buffers[-1]
    wait = prepare(given, buffers, wt, wot, cols, keep, sems)

    def body(group, _):
        wait(group)
        spread(tiles, x, group)

        def pair(q, _):
            n, col = group * PAIRS + q, group * GROUP + q
            for part in range(3):
                centred, inv = centre(gather(x, 0, q, part))
                unit_z = centred * inv
                nz = (unit_z * cols[0] + cols[1]).astype(BF16)
                kept_by = keep_of(keep, col, part)
                for m in (0, 1):
                    gate = jnp.tanh(dot(wt[2 * m + 1], nz))
                    kept = (gate + 1.0) * kept_by
                    saved_ref[n, part, 2 * m] = kept.astype(BF16)
                    saved_ref[n, part, 2 * m + 1] = (kept * dot(wt[2 * m], nz) * (0.5 - 0.5 * gate)).astype(BF16)
                gate = jnp.tanh(dot(wt[4], nz))
                centred, inv_x = centre(gather(x, 1, q, part))
                nx = (centred * inv_x * cols[2] + cols[3]).astype(BF16)
                slope = (0.5 + 0.5 * gate) * (0.5 - 0.5 * gate)
                saved_ref[n, part, 4] = (gather(x, 2, q, part) * dot(wot[...], nx) * slope).astype(BF16)
                saved_ref[n, part, 5] = unit_z.astype(BF16)
                inv_ref[n, part] = jnp.broadcast_to(inv, (8, C))
            return 0

        lax.fori_loop(0, PAIRS, pair, 0)
        return 0

    lax.fori_loop(0, GROUPS, body, 0)


def channel_kernel(in_v, out_ref, g, left, right, out_v, sems):
    low8, low16, low24 = (low_lanes((n, C)) for n in (GROUP, TAIL, COLS))

    def take(w):
        blocks = [in_v[w * 4 + h].astype(F32) for h in range(4)]

        def part(n):
            at = [STEP * m + GROUP * n for m in range(3)]
            return [jnp.concatenate([b[a : a + GROUP] for a in at], 0) for b in blocks]

        rows_g, rows_l, rows_r, mixed = part(0), part(1), part(2), part(3)
        for h in (0, 2):
            a, b = blocks[h][TAIL_AT:], blocks[h + 1][TAIL_AT:]
            one, two = jnp.where(low16, a, swap(b)), jnp.where(low16, swap(a), b)
            pieces = [v[PAIRS * m : PAIRS * (m + 1)] for m in range(3) for v in (one, two)]
            rows_g.append(jnp.concatenate(pieces, 0))
            a, b = mixed[h], mixed[h + 1]
            rows_l.append(jnp.where(low24, a, swap(b)))
            rows_r.append(jnp.where(low24, swap(a), b))
        return [jnp.concatenate(rows, 1) for rows in (rows_g, rows_l, rows_r)]

    def move(pair):
        one, two = take(2 * pair), take(2 * pair + 1)
        at = pl.ds(pl.multiple_of(pair * 48, 16), 48)
        both = [jnp.concatenate([a, b], 0).astype(BF16) for a, b in zip(one, two)]
        left[at, :] = both[1]
        right[at, :] = both[2]
        for n in range(3):
            block = pair * 3 + n
            half = block // 12
            rest = block - half * 12
            to = jnp.where(rest < 8, half * 8 + rest, 32 + half * 4 + rest - 8)
            g[pl.ds(pl.multiple_of(to * 16, 16), 16), :] = both[0][n * 16 : (n + 1) * 16]

    def body(n, _):
        for pair in range(16 // FETCHES):
            move(n * (16 // FETCHES) + pair)
        return 0

    lax.fori_loop(0, FETCHES, body, 0)

    def send(n):
        part = pl.ds(n * (C // CHUNKS), C // CHUNKS)
        return pltpu.make_async_copy(out_v.at[part], out_ref.at[part], sems.at[n])

    for n in range(CHUNKS):
        rows = slice(n * CHUNK, (n + 1) * CHUNK)
        back_l = dot(right[rows, :], g[...])
        back_r = lax.dot_general(left[rows, :], g[...], (((1,), (1,)), ((), ())), preferred_element_type=F32)
        for w in range(CHUNK // COLS):
            for h in range(4):
                lanes, tail = slice(h * C, (h + 1) * C), slice((4 + h // 2) * C, (5 + h // 2) * C)
                pieces = []
                for m in range(3):
                    at = slice(w * COLS + m * GROUP, w * COLS + (m + 1) * GROUP)
                    a, b = back_l[at, tail], back_r[at, tail]
                    mixed = jnp.where(low8, a, swap(b)) if h % 2 == 0 else jnp.where(low8, swap(a), b)
                    pieces += [back_l[at, lanes], back_r[at, lanes], mixed]
                out_v[(n * (CHUNK // COLS) + w) * 4 + h] = jnp.concatenate(pieces, 0).astype(BF16)
        send(n).start()
    for n in range(CHUNKS):
        send(n).wait()


def back_kernel(
    in_ref, saved_ref, inv_ref, w_ref, gain_ref, out_ref,
    in_v, saved_v, inv_v, w_v, gain_v, rows, cols, stage, out_v, in_sems, sems, out_sems,
):

    def fetch(n):
        at = pl.ds(pl.multiple_of(n * BACK_STEP, 8), BACK_STEP)
        return pltpu.make_async_copy(in_ref.at[:, at], in_v.at[n], in_sems.at[n])

    started = copies([w_ref, gain_ref, inv_ref], [w_v, gain_v, inv_v], sems)

    def take(group):
        at = pl.ds(group * PAIRS, PAIRS)
        return pltpu.make_async_copy(saved_ref.at[at], saved_v.at[at], sems.at[3 + group])

    for group in range(GROUPS):
        fetch(group).start()
        take(group).start()
    low = low_lanes((C, C))

    def send(group):
        at = pl.ds(pl.multiple_of(group * GROUP, GROUP), GROUP)
        return pltpu.make_async_copy(out_v.at[group], out_ref.at[:, at], out_sems.at[group])

    for copy in started:
        copy.wait()
    cols[...] = column(gain_v)

    def body(group, _):
        fetch(group).wait()

        def fill(c, _):
            rows[pl.ds(c * BACK_PITCH, BACK_STEP), :] = in_v[group, c].astype(F32)
            return 0

        lax.fori_loop(0, C, fill, 0, unroll=8)
        take(group).wait()

        def get(row):
            return rows[pl.ds(row, C, stride=BACK_PITCH), :]

        def put(row, value):
            stage[pl.ds(row, value.shape[0], stride=X_PITCH), :] = value

        for q in range(PAIRS):
            n = group * PAIRS + q
            a, b = get(2 * GROUP + q), get(2 * GROUP + PAIRS + q)
            lefts = [get(q), get(PAIRS + q), jnp.where(low, a, swap(b))]
            rights = [get(GROUP + q), get(GROUP + PAIRS + q), jnp.where(low, swap(a), b)]
            for part in range(3):
                saved = saved_v.at[n, part]
                grad_l, grad_r = lefts[part].astype(BF16), rights[part].astype(BF16)
                pieces = [grad_l * saved[0], grad_l * saved[1], grad_r * saved[2], grad_r * saved[3], saved[4]]
                e = dot(w_v[...], jnp.concatenate(pieces, 0)) * cols[...]
                unit_z = saved[5].astype(F32)
                grad = (inv_v[n, part][:1] * (e - mean(e) - unit_z * mean(e * unit_z))).T
                if part < 2:
                    put(q + PAIRS * part, grad)
                else:
                    put(C * X_PITCH + q, grad[:64])
                    put(C * X_PITCH + PAIRS + q, grad[64:])

        def flush(i, _):
            found = [stage[pl.ds((i * 16 + m) * X_PITCH, GROUP), :].reshape(1, GROUP, C) for m in range(16)]
            out_v[group, pl.ds(i * 16, 16)] = jnp.concatenate(found, 0).astype(BF16)
            return 0

        lax.fori_loop(0, ROWS // 16, flush, 0, unroll=2)
        send(group).start()
        return 0

    lax.fori_loop(0, GROUPS, body, 0)
    for group in range(GROUPS):
        send(group).wait()


HBM = pl.BlockSpec(memory_space=pltpu.HBM)
VMEM = pl.BlockSpec(memory_space=pltpu.VMEM)


def call(kernel, ins, outs, out_specs, scratch, args, limit, flops, moved):
    return pl.pallas_call(
        kernel,
        out_shape=outs,
        in_specs=ins,
        out_specs=out_specs,
        scratch_shapes=scratch,
        compiler_params=pltpu.CompilerParams(vmem_limit_bytes=limit << 20),
        cost_estimate=pl.CostEstimate(flops=flops, bytes_accessed=moved, transcendentals=0),
    )(*args)


def exchange(x):
    return lax.all_to_all(x, AXES, split_axis=0, concat_axis=0, tiled=True)


def on_device(*given):
    shape, vmem, dma = jax.ShapeDtypeStruct, pltpu.VMEM, pltpu.SemaphoreType.DMA
    in_weight, in_gain = given[6], given[8]
    buffers = [
        *(vmem(v.shape, v.dtype) for v in given[3:]),
        vmem((GROUPS, 3, ROWS, GROUP, C), BF16),
        vmem((3, X_SIZE, C), F32),
        vmem((5, C, C), BF16),
        vmem((C, C), BF16),
        vmem((5, C, C), F32),
        vmem((2, COLS, C), F32),
    ]
    sent = call(
        front_kernel,
        [HBM] * 12,
        shape((C, OUT_ROWS, C), BF16),
        HBM,
        [
            *buffers,
            vmem((OUT_SIZE, C), F32),
            vmem((C * TAIL_PITCH, C), F32),
            vmem((C, OUT_ROWS, C), BF16),
            dma((18,)),
            dma((GROUPS,)),
        ],
        given,
        66,
        2 * 4608 * 128 * 768,
        8 << 20,
    )
    saved, inv = call(
        save_kernel,
        [HBM] * 12,
        (shape((GROUPS * PAIRS, 3, 6, C, C), BF16), shape((GROUPS * PAIRS, 3, 8, C), F32)),
        (VMEM, VMEM),
        [*buffers, dma((18,))],
        given,
        66,
        2 * 4608 * 128 * 768,
        12 << 20,
    )
    got = exchange(sent)
    square = vmem((RES, RES), BF16)
    back = call(
        channel_kernel,
        [VMEM],
        shape((C, BACK_ROWS, C), BF16),
        HBM,
        [
            square,
            square,
            square,
            vmem((C, BACK_ROWS, C), BF16),
            dma((CHUNKS,)),
        ],
        [got],
        40,
        4 * RES**3,
        8 << 20,
    )
    returned = exchange(back)
    return call(
        back_kernel,
        [HBM] * 5,
        shape((ROWS, COLS, C), BF16),
        HBM,
        [
            vmem((GROUPS, C, BACK_STEP, C), BF16),
            vmem(saved.shape, BF16),
            vmem(inv.shape, F32),
            vmem(in_weight.shape, BF16),
            vmem(in_gain.shape, F32),
            vmem((BACK_SIZE, C), F32),
            vmem((C, C), F32),
            vmem((X_SIZE, C), F32),
            vmem((GROUPS, ROWS, GROUP, C), BF16),
            dma((GROUPS,)),
            dma((3 + GROUPS,)),
            dma((GROUPS,)),
        ],
        [returned, saved, inv, in_weight, in_gain],
        66,
        2 * 4608 * 128 * 640,
        12 << 20,
    )


def solution(mesh):
    return jax.shard_map(
        on_device,
        mesh=mesh,
        in_specs=(P("half", "ch", None),) * 3 + (P(),) * 9,
        out_specs=P("half", "ch", None),
        check_vma=False,
    )
```

time: 365 us -> 117 us (0.32)
  waiting for transfers between devices: 187 us -> 22.2 us
  local copies, waits for them, and re-layouts: 45.2 us -> 0 us
  blocking collectives: 28.1 us -> 59 us
  other arithmetic: 30.3 us -> 0 us
  starting transfers between devices: 35.5 us -> 5.51 us
  Pallas kernels: 0 us -> 29.5 us
  matrix products: 23 us -> 0 us
  between operations: 14.5 us -> 0.03 us
    unnamed x3 -> x0, waiting for transfers between devices: 82.9 us -> none
    all_gather x1 -> x0, waiting for transfers between devices: 56.1 us -> none  [on_device(): lax.all_gather(right_ch, 'half', axis=0, tiled=True)]
    all_to_all x1, blocking collectives: 28.1 us -> 59 us  [exchange(): return lax.all_to_all(x, AXES, split_axis=0, concat_axis=0, tiled=True)]
    all_to_all x4 -> x1, starting transfers between devices: 35.2 us -> 5.51 us  [exchange(): return lax.all_to_all(x, AXES, split_axis=0, concat_axis=0, tiled=True)]
    pallas_call x0 -> x4, Pallas kernels: none -> 29.5 us  [call(): pl.pallas_call(kernel, out_shape=outs, in_specs=ins, out_specs=out_specs,...]
    all_to_all x4 -> x1, waiting for transfers between devices: 48.3 us -> 22.2 us  [exchange(): return lax.all_to_all(x, AXES, split_axis=0, concat_axis=0, tiled=True)]
    dot_general x7 -> x0, matrix products: 23 us -> none  [the longest x1 4.48 us: on_device(): jnp.einsum('icj,jck->ick', grad_block, lax.all_gather(right_ch, 'half', a...]
    convert_element_type x6 -> x0, local copies, waits for them, and re-layouts: 22.2 us -> none  [the longest x1 8.52 us: on_device(): jnp.einsum('icj,ick->jck', grad_block, left_ch, preferred_element_type=jn...]
  transfers between devices with their start and end apart: 6 -> 1, of which waited for: 5 -> 1; matrix products, arithmetic and copies ran while one was open for 10% -> 0% of each run, Pallas kernels for 0% -> 9%
where the time goes in v4:
time: 117 us; the launch traced here: 116 us
  blocking collectives  59 us (50%)
  Pallas kernels  29.5 us (25%)
  waiting for transfers between devices  22.2 us (19%)
  starting transfers between devices  5.51 us (5%)
    all_to_all x1, blocking collectives, exchange(): return lax.all_to_all(x, AXES, split_axis=0, concat_axis=0, tiled=True)  59 us
    pallas_call x4, Pallas kernels, call(): pl.pallas_call(kernel, out_shape=outs, in_specs=ins, out_specs=out_specs,...  29.5 us
    all_to_all x1, waiting for transfers between devices, exchange(): return lax.all_to_all(x, AXES, split_axis=0, concat_axis=0, tiled=True)  22.2 us
    all_to_all x1, starting transfers between devices, exchange(): return lax.all_to_all(x, AXES, split_axis=0, concat_axis=0, tiled=True)  5.51 us
  transfers between devices with their start and end apart: 1, of which 1 were waited for; matrix products, arithmetic and copies ran while one was open for 0% of the time, Pallas kernels for 9%

profile of v4, /device:TPU:1, one launch (start us, length us, event | category | flops | bytes accessed | tf_op | source)
XLA Modules:
  0.0 116.3 jit_solution(15117045557318693691)
XLA Ops:
  0.0 8.2 %shard_map.118 = bf16[128,112,128]{2,1,0:T(8,128)(2,1)} custom-call(bf16[192,24,128]{2,1,0:T(8,128)(2,1)} %refs_0_.3, bf16[192,24,128]{2,1,0:T(8,128)(2,1)} %refs_1_.3, bf16[192,24,128]{2,1,0:T(8,128)(2,1)} %refs_2_.3, s32[768]{0:T(1024)} %refs_3_.3, s32[768]{0:T(1024)} %refs_4_.3, s32[4,4]{1,0:T(4,128)} %refs_5_.3, bf16[128,640]{1,0:T(8,128)(2,1)} %w_ref.1, ...), custom_call_target="tpu_custom_call" | custom-call | flops 905969664 | bytes 8388608 | tf_op jit(solution)/shard_map/pallas_call | solution.py:381
  8.2 59.0 %all_to_all.10.in_v = bf16[128,112,128]{2,1,0:T(8,128)(2,1)S(1)} all-to-all(bf16[128,112,128]{2,1,0:T(8,128)(2,1)} %shard_map.118), channel_id=1, replica_groups=mesh['ch'=32,'half'=4] {'ch','half'}, dimensions={0} | all-to-all | bytes 7340032 | tf_op jit(solution)/shard_map/all_to_all | solution.py:393
  67.3 4.4 %shard_map.119 = bf16[128,72,128]{2,1,0:T(8,128)(2,1)} custom-call(bf16[128,112,128]{2,1,0:T(8,128)(2,1)S(1)} %all_to_all.10.in_v), custom_call_target="tpu_custom_call" | custom-call | flops 1811939328 | bytes 8388608 | tf_op jit(solution)/shard_map/pallas_call | solution.py:381
  71.7 5.5 %all-to-all-start.1 = ((bf16[128,72,128]{2,1,0:T(8,128)(2,1)}), bf16[128,72,128]{2,1,0:T(8,128)(2,1)}, u32[]{:S(2)}, u32[]{:S(2)}) async-start(bf16[128,72,128]{2,1,0:T(8,128)(2,1)} %shard_map.119), calls=%async_computation.1 | async-start | bytes 4718592 | tf_op jit(solution)/shard_map/all_to_all | solution.py:393
  77.2 10.9 %shard_map.120 = (bf16[12,3,6,128,128]{4,3,2,1,0:T(8,128)(2,1)}, f32[12,3,8,128]{3,2,1,0:T(8,128)}) custom-call(bf16[192,24,128]{2,1,0:T(8,128)(2,1)} %refs_0_.3, bf16[192,24,128]{2,1,0:T(8,128)(2,1)} %refs_1_.3, bf16[192,24,128]{2,1,0:T(8,128)(2,1)} %refs_2_.3, s32[768]{0:T(1024)} %refs_3_.3, s32[768]{0:T(1024)} %refs_4_.3, s32[4,4]{1,0:T(4,128)} %refs_5_.3, ...), custom_call_target="tpu_custom_call" | custom-call | flops 905969664 | bytes 12582912 | tf_op jit(solution)/shard_map/pallas_call | solution.py:381
  88.1 22.2 %all-to-all-done.1.in_ref = bf16[128,72,128]{2,1,0:T(8,128)(2,1)} async-done(((bf16[128,72,128]{2,1,0:T(8,128)(2,1)}), bf16[128,72,128]{2,1,0:T(8,128)(2,1)}, u32[]{:S(2)}, u32[]{:S(2)}) %all-to-all-start.1) | async-done | bytes 2359328 | tf_op jit(solution)/shard_map/all_to_all | solution.py:393
  110.4 6.0 %shard_map.121 = bf16[192,24,128]{2,1,0:T(8,128)(2,1)} custom-call(bf16[128,72,128]{2,1,0:T(8,128)(2,1)} %all-to-all-done.1.in_ref, bf16[12,3,6,128,128]{4,3,2,1,0:T(8,128)(2,1)} %get-tuple-element.7.saved_ref, f32[12,3,8,128]{3,2,1,0:T(8,128)} %get-tuple-element.8.inv_ref, bf16[128,640]{1,0:T(8,128)(2,1)} %w_ref.1, f32[128]{0:T(128)} %gain_ref.1), custom_call_target="tpu_custom_call" | custom-call | flops 754974720 | bytes 12582912 | tf_op jit(solution)/shard_map/pallas_call | solution.py:381
Async XLA Ops:
  71.7 38.7 %all-to-all-start.1 = ((bf16[128,72,128]{2,1,0:T(8,128)(2,1)}), bf16[128,72,128]{2,1,0:T(8,128)(2,1)}, u32[]{:S(2)}, u32[]{:S(2)}) async-start(bf16[128,72,128]{2,1,0:T(8,128)(2,1)} %shard_map.119), calls=%async_computation.1 | async-start | bytes 4718592 | tf_op jit(solution)/shard_map/all_to_all | solution.py:393

commit v5 on v4

--- a/solution.py
+++ b/solution.py
@@ -17,7 +17,7 @@
 X_PITCH, OUT_PITCH, TAIL_PITCH, BACK_PITCH = GROUP + 1, STEP + 1, TAIL + 1, BACK_STEP + 1
 X_SIZE, OUT_SIZE, BACK_SIZE = ROWS * X_PITCH, C * OUT_PITCH, C * BACK_PITCH
 FETCHES = 8
-CHUNKS = 4
+CHUNKS = 2
 CHUNK = RES // CHUNKS
 
 
@@ -53,8 +53,9 @@
     return started
 
 
-def spread(tiles, x, group):
+def spread(tiles, x, group, wait):
     for n in range(3):
+        wait(group, n)
 
         def body(i, _):
             values = tiles[group, n, pl.ds(pl.multiple_of(i * 16, 16), 16)].astype(F32)
@@ -62,7 +63,7 @@
                 x[n, pl.ds((i * 16 + m) * X_PITCH, GROUP), :] = values[m]
             return 0
 
-        lax.fori_loop(0, ROWS // 16, body, 0, unroll=2)
+        lax.fori_loop(0, ROWS // 16, body, 0, unroll=12)
 
 
 def gather(x, n, q, part):
@@ -119,11 +120,7 @@
     cols[4] = cols[2] * 0.5
     find_keep(mask_v, chain_v, pairs_v, keep)
 
-    def wait(group):
-        for n in range(3):
-            tile(group, n).wait()
-
-    return wait
+    return lambda group, n: tile(group, n).wait()
 
 
 def front_kernel(*refs):
@@ -139,8 +136,7 @@
         return pltpu.make_async_copy(packed.at[:, rows], out_ref.at[:, rows], out_sems.at[group])
 
     def body(group, _):
-        wait(group)
-        spread(tiles, x, group)
+        spread(tiles, x, group, wait)
         for q in range(PAIRS):
             col = group * GROUP + q
 
@@ -173,7 +169,8 @@
             packed[c, rows] = stage[pl.ds(c * OUT_PITCH, STEP), :].astype(BF16)
             return 0
 
-        lax.fori_loop(0, C, pack, 0, unroll=8)
+        for c in range(C):
+            pack(c, 0)
 
         @pl.when(group < GROUPS - 1)
         def _():
@@ -187,7 +184,8 @@
         packed[c, TAIL_AT:] = stage_tail[pl.ds(c * TAIL_PITCH, TAIL), :].astype(BF16)
         return 0
 
-    lax.fori_loop(0, C, pack, 0, unroll=8)
+    for c in range(C):
+        pack(c, 0)
     rest = pl.ds((GROUPS - 1) * STEP, OUT_ROWS - (GROUPS - 1) * STEP)
     final = pltpu.make_async_copy(packed.at[:, rest], out_ref.at[:, rest], out_sems.at[GROUPS - 1])
     final.start()
@@ -203,8 +201,7 @@
     wait = prepare(given, buffers, wt, wot, cols, keep, sems)
 
     def body(group, _):
-        wait(group)
-        spread(tiles, x, group)
+        spread(tiles, x, group, wait)
 
         def pair(q, _):
             n, col = group * PAIRS + q, group * GROUP + q
@@ -272,7 +269,7 @@
             move(n * (16 // FETCHES) + pair)
         return 0
 
-    lax.fori_loop(0, FETCHES, body, 0)
+    lax.fori_loop(0, FETCHES, body, 0, unroll=2)
 
     def send(n):
         part = pl.ds(n * (C // CHUNKS), C // CHUNKS)
@@ -332,7 +329,8 @@
             rows[pl.ds(c * BACK_PITCH, BACK_STEP), :] = in_v[group, c].astype(F32)
             return 0
 
-        lax.fori_loop(0, C, fill, 0, unroll=8)
+        for c in range(C):
+            fill(c, 0)
         take(group).wait()
 
         def get(row):
@@ -364,7 +362,7 @@
             out_v[group, pl.ds(i * 16, 16)] = jnp.concatenate(found, 0).astype(BF16)
             return 0
 
-        lax.fori_loop(0, ROWS // 16, flush, 0, unroll=2)
+        lax.fori_loop(0, ROWS // 16, flush, 0, unroll=12)
         send(group).start()
         return 0
 

time: 117 us -> 115 us (0.983)
  Pallas kernels: 29.5 us -> 27.7 us
    pallas_call x4, Pallas kernels: 29.5 us -> 27.7 us  [call(): pl.pallas_call(kernel, out_shape=outs, in_specs=ins, out_specs=out_specs,...]
where the time goes in v5:
time: 115 us
  blocking collectives  59 us (51%)
  Pallas kernels  27.7 us (24%)
  waiting for transfers between devices  22.5 us (20%)
  starting transfers between devices  5.52 us (5%)
    all_to_all x1, blocking collectives, exchange(): return lax.all_to_all(x, AXES, split_axis=0, concat_axis=0, tiled=True)  59 us
    pallas_call x4, Pallas kernels, call(): pl.pallas_call(kernel, out_shape=outs, in_specs=ins, out_specs=out_specs,...  27.7 us
    all_to_all x1, waiting for transfers between devices, exchange(): return lax.all_to_all(x, AXES, split_axis=0, concat_axis=0, tiled=True)  22.5 us
    all_to_all x1, starting transfers between devices, exchange(): return lax.all_to_all(x, AXES, split_axis=0, concat_axis=0, tiled=True)  5.52 us
  transfers between devices with their start and end apart: 1, of which 1 were waited for; matrix products, arithmetic and copies ran while one was open for 0% of the time, Pallas kernels for 9%

profile of v5, /device:TPU:1, one launch (start us, length us, event | category | flops | bytes accessed | tf_op | source)
XLA Modules:
  0.0 114.8 jit_solution(1042388012319697435)
XLA Ops:
  0.0 7.4 %shard_map.118 = bf16[128,112,128]{2,1,0:T(8,128)(2,1)} custom-call(bf16[192,24,128]{2,1,0:T(8,128)(2,1)} %refs_0_.3, bf16[192,24,128]{2,1,0:T(8,128)(2,1)} %refs_1_.3, bf16[192,24,128]{2,1,0:T(8,128)(2,1)} %refs_2_.3, s32[768]{0:T(1024)} %refs_3_.3, s32[768]{0:T(1024)} %refs_4_.3, s32[4,4]{1,0:T(4,128)} %refs_5_.3, bf16[128,640]{1,0:T(8,128)(2,1)} %w_ref.1, ...), custom_call_target="tpu_custom_call" | custom-call | flops 905969664 | bytes 8388608 | tf_op jit(solution)/shard_map/pallas_call | solution.py:379
  7.4 59.0 %all_to_all.10.in_v = bf16[128,112,128]{2,1,0:T(8,128)(2,1)S(1)} all-to-all(bf16[128,112,128]{2,1,0:T(8,128)(2,1)} %shard_map.118), channel_id=1, replica_groups=mesh['ch'=32,'half'=4] {'ch','half'}, dimensions={0} | all-to-all | bytes 7340032 | tf_op jit(solution)/shard_map/all_to_all | solution.py:391
  66.4 3.9 %shard_map.119 = bf16[128,72,128]{2,1,0:T(8,128)(2,1)} custom-call(bf16[128,112,128]{2,1,0:T(8,128)(2,1)S(1)} %all_to_all.10.in_v), custom_call_target="tpu_custom_call" | custom-call | flops 1811939328 | bytes 8388608 | tf_op jit(solution)/shard_map/pallas_call | solution.py:379
  70.4 5.5 %all-to-all-start.1 = ((bf16[128,72,128]{2,1,0:T(8,128)(2,1)}), bf16[128,72,128]{2,1,0:T(8,128)(2,1)}, u32[]{:S(2)}, u32[]{:S(2)}) async-start(bf16[128,72,128]{2,1,0:T(8,128)(2,1)} %shard_map.119), calls=%async_computation.1 | async-start | bytes 4718592 | tf_op jit(solution)/shard_map/all_to_all | solution.py:391
  75.9 10.7 %shard_map.120 = (bf16[12,3,6,128,128]{4,3,2,1,0:T(8,128)(2,1)}, f32[12,3,8,128]{3,2,1,0:T(8,128)}) custom-call(bf16[192,24,128]{2,1,0:T(8,128)(2,1)} %refs_0_.3, bf16[192,24,128]{2,1,0:T(8,128)(2,1)} %refs_1_.3, bf16[192,24,128]{2,1,0:T(8,128)(2,1)} %refs_2_.3, s32[768]{0:T(1024)} %refs_3_.3, s32[768]{0:T(1024)} %refs_4_.3, s32[4,4]{1,0:T(4,128)} %refs_5_.3, ...), custom_call_target="tpu_custom_call" | custom-call | flops 905969664 | bytes 12582912 | tf_op jit(solution)/shard_map/pallas_call | solution.py:379
  86.6 22.5 %all-to-all-done.1.in_ref = bf16[128,72,128]{2,1,0:T(8,128)(2,1)} async-done(((bf16[128,72,128]{2,1,0:T(8,128)(2,1)}), bf16[128,72,128]{2,1,0:T(8,128)(2,1)}, u32[]{:S(2)}, u32[]{:S(2)}) %all-to-all-start.1) | async-done | bytes 2359328 | tf_op jit(solution)/shard_map/all_to_all | solution.py:391
  109.0 5.7 %shard_map.121 = bf16[192,24,128]{2,1,0:T(8,128)(2,1)} custom-call(bf16[128,72,128]{2,1,0:T(8,128)(2,1)} %all-to-all-done.1.in_ref, bf16[12,3,6,128,128]{4,3,2,1,0:T(8,128)(2,1)} %get-tuple-element.7.saved_ref, f32[12,3,8,128]{3,2,1,0:T(8,128)} %get-tuple-element.8.inv_ref, bf16[128,640]{1,0:T(8,128)(2,1)} %w_ref.1, f32[128]{0:T(128)} %gain_ref.1), custom_call_target="tpu_custom_call" | custom-call | flops 754974720 | bytes 12582912 | tf_op jit(solution)/shard_map/pallas_call | solution.py:379
Async XLA Ops:
  70.4 38.7 %all-to-all-start.1 = ((bf16[128,72,128]{2,1,0:T(8,128)(2,1)}), bf16[128,72,128]{2,1,0:T(8,128)(2,1)}, u32[]{:S(2)}, u32[]{:S(2)}) async-start(bf16[128,72,128]{2,1,0:T(8,128)(2,1)} %shard_map.119), calls=%async_computation.1 | async-start | bytes 4718592 | tf_op jit(solution)/shard_map/all_to_all | solution.py:391

commit v6 on v5

--- a/solution.py
+++ b/solution.py
@@ -17,8 +17,10 @@
 X_PITCH, OUT_PITCH, TAIL_PITCH, BACK_PITCH = GROUP + 1, STEP + 1, TAIL + 1, BACK_STEP + 1
 X_SIZE, OUT_SIZE, BACK_SIZE = ROWS * X_PITCH, C * OUT_PITCH, C * BACK_PITCH
 FETCHES = 8
+ENDS = 4
 CHUNKS = 2
 CHUNK = RES // CHUNKS
+SENT = 4
 
 
 def dot(a, b):
@@ -114,8 +116,7 @@
     for n in range(5):
         part = w_v[:, n * C : (n + 1) * C].astype(F32).T
         wt[n] = (part * 0.5 if n in (1, 3, 4) else part).astype(BF16)
-    wot[...] = wo_v[...].astype(F32).T.astype(BF16)
-    for n, g in enumerate(gains):
+    for n, g in enumerate(gains[:3]):
         cols[n] = column(g)
     cols[4] = cols[2] * 0.5
     find_keep(mask_v, chain_v, pairs_v, keep)
@@ -134,6 +135,10 @@
     def send(group):
         rows = pl.ds(pl.multiple_of(group * STEP, STEP), STEP)
         return pltpu.make_async_copy(packed.at[:, rows], out_ref.at[:, rows], out_sems.at[group])
+
+    def pack(c, group):
+        rows = pl.ds(pl.multiple_of(group * STEP, STEP), STEP)
+        packed[c, rows] = stage[pl.ds(c * OUT_PITCH, STEP), :].astype(BF16)
 
     def body(group, _):
         spread(tiles, x, group, wait)
@@ -164,34 +169,30 @@
                     put(3 * GROUP + q, jnp.where(low, left, swap(right)))
                     put(3 * GROUP + PAIRS + q, jnp.where(low, swap(left), right))
 
-        def pack(c, _):
-            rows = pl.ds(pl.multiple_of(group * STEP, STEP), STEP)
-            packed[c, rows] = stage[pl.ds(c * OUT_PITCH, STEP), :].astype(BF16)
-            return 0
-
-        for c in range(C):
-            pack(c, 0)
-
         @pl.when(group < GROUPS - 1)
         def _():
+            for c in range(C):
+                pack(c, group)
             send(group).start()
 
         return 0
 
     lax.fori_loop(0, GROUPS, body, 0)
-
-    def pack(c, _):
+    last = GROUPS - 1
+
+    def send_last(n):
+        part, rest = pl.ds(n * (C // ENDS), C // ENDS), pl.ds(last * STEP, OUT_ROWS - last * STEP)
+        return pltpu.make_async_copy(packed.at[part, rest], out_ref.at[part, rest], out_sems.at[last + n])
+
+    for c in range(C):
+        pack(c, last)
         packed[c, TAIL_AT:] = stage_tail[pl.ds(c * TAIL_PITCH, TAIL), :].astype(BF16)
-        return 0
-
-    for c in range(C):
-        pack(c, 0)
-    rest = pl.ds((GROUPS - 1) * STEP, OUT_ROWS - (GROUPS - 1) * STEP)
-    final = pltpu.make_async_copy(packed.at[:, rest], out_ref.at[:, rest], out_sems.at[GROUPS - 1])
-    final.start()
-    for group in range(GROUPS - 1):
+        if (c + 1) % (C // ENDS) == 0:
+            send_last(c // (C // ENDS)).start()
+    for group in range(last):
         send(group).wait()
-    final.wait()
+    for n in range(ENDS):
+        send_last(n).wait()
 
 
 def save_kernel(*refs):
@@ -199,6 +200,8 @@
     *buffers, x, wt, wot, cols, keep, sems = refs[14:]
     tiles = buffers[-1]
     wait = prepare(given, buffers, wt, wot, cols, keep, sems)
+    wot[...] = buffers[4][...].astype(F32).T.astype(BF16)
+    cols[3] = column(buffers[8])
 
     def body(group, _):
         spread(tiles, x, group, wait)
@@ -272,7 +275,7 @@
     lax.fori_loop(0, FETCHES, body, 0, unroll=2)
 
     def send(n):
-        part = pl.ds(n * (C // CHUNKS), C // CHUNKS)
+        part = pl.ds(n * 4 * SENT, 4 * SENT)
         return pltpu.make_async_copy(out_v.at[part], out_ref.at[part], sems.at[n])
 
     for n in range(CHUNKS):
@@ -289,8 +292,9 @@
                     mixed = jnp.where(low8, a, swap(b)) if h % 2 == 0 else jnp.where(low8, swap(a), b)
                     pieces += [back_l[at, lanes], back_r[at, lanes], mixed]
                 out_v[(n * (CHUNK // COLS) + w) * 4 + h] = jnp.concatenate(pieces, 0).astype(BF16)
-        send(n).start()
-    for n in range(CHUNKS):
+            if w % SENT == SENT - 1:
+                send((n * (CHUNK // COLS) + w) // SENT).start()
+    for n in range(32 // SENT):
         send(n).wait()
 
 
@@ -344,15 +348,22 @@
             a, b = get(2 * GROUP + q), get(2 * GROUP + PAIRS + q)
             lefts = [get(q), get(PAIRS + q), jnp.where(low, a, swap(b))]
             rights = [get(GROUP + q), get(GROUP + PAIRS + q), jnp.where(low, swap(a), b)]
-            for part in range(3):
-                saved = saved_v.at[n, part]
-                grad_l, grad_r = lefts[part].astype(BF16), rights[part].astype(BF16)
-                pieces = [grad_l * saved[0], grad_l * saved[1], grad_r * saved[2], grad_r * saved[3], saved[4]]
-                e = dot(w_v[...], jnp.concatenate(pieces, 0)) * cols[...]
-                unit_z = saved[5].astype(F32)
-                grad = (inv_v[n, part][:1] * (e - mean(e) - unit_z * mean(e * unit_z))).T
-                if part < 2:
-                    put(q + PAIRS * part, grad)
+            for parts in ((0, 1), (2,)):
+
+                def wide(take_one):
+                    return jnp.concatenate([take_one(part) for part in parts], 1)
+
+                grad_l = wide(lambda part: lefts[part].astype(BF16))
+                grad_r = wide(lambda part: rights[part].astype(BF16))
+                s0, s1, s2, s3, s4, s5 = (wide(lambda part, m=m: saved_v[n, part, m]) for m in range(6))
+                pieces = [grad_l * s0, grad_l * s1, grad_r * s2, grad_r * s3, s4]
+                e = dot(w_v[...], jnp.concatenate(pieces, 0)) * wide(lambda part: cols[...])
+                unit_z = s5.astype(F32)
+                inv = wide(lambda part: inv_v[n, part][:1])
+                grad = (inv * (e - mean(e) - unit_z * mean(e * unit_z))).T
+                if parts != (2,):
+                    put(q, grad[:C])
+                    put(q + PAIRS, grad[C:])
                 else:
                     put(C * X_PITCH + q, grad[:64])
                     put(C * X_PITCH + PAIRS + q, grad[64:])
@@ -414,7 +425,7 @@
             vmem((C * TAIL_PITCH, C), F32),
             vmem((C, OUT_ROWS, C), BF16),
             dma((18,)),
-            dma((GROUPS,)),
+            dma((GROUPS - 1 + ENDS,)),
         ],
         given,
         66,
@@ -444,7 +455,7 @@
             square,
             square,
             vmem((C, BACK_ROWS, C), BF16),
-            dma((CHUNKS,)),
+            dma((32 // SENT,)),
         ],
         [got],
         40,

time: 115 us -> 115 us (level)
  no operation moved by 1% of the time
where the time goes in v6:
time: 115 us
  blocking collectives  59 us (51%)
  Pallas kernels  27.7 us (24%)
  waiting for transfers between devices  22.5 us (20%)
  starting transfers between devices  5.53 us (5%)
    all_to_all x1, blocking collectives, exchange(): return lax.all_to_all(x, AXES, split_axis=0, concat_axis=0, tiled=True)  59 us
    pallas_call x4, Pallas kernels, call(): pl.pallas_call(kernel, out_shape=outs, in_specs=ins, out_specs=out_specs,...  27.7 us
    all_to_all x1, waiting for transfers between devices, exchange(): return lax.all_to_all(x, AXES, split_axis=0, concat_axis=0, tiled=True)  22.5 us
    all_to_all x1, starting transfers between devices, exchange(): return lax.all_to_all(x, AXES, split_axis=0, concat_axis=0, tiled=True)  5.53 us
  transfers between devices with their start and end apart: 1, of which 1 were waited for; matrix products, arithmetic and copies ran while one was open for 0% of the time, Pallas kernels for 9%

profile of v6, /device:TPU:1, one launch (start us, length us, event | category | flops | bytes accessed | tf_op | source)
XLA Modules:
  0.0 114.8 jit_solution(7391147996839701563)
XLA Ops:
  0.0 7.4 %shard_map.118 = bf16[128,112,128]{2,1,0:T(8,128)(2,1)} custom-call(bf16[192,24,128]{2,1,0:T(8,128)(2,1)} %refs_0_.3, bf16[192,24,128]{2,1,0:T(8,128)(2,1)} %refs_1_.3, bf16[192,24,128]{2,1,0:T(8,128)(2,1)} %refs_2_.3, s32[768]{0:T(1024)} %refs_3_.3, s32[768]{0:T(1024)} %refs_4_.3, s32[4,4]{1,0:T(4,128)} %refs_5_.3, bf16[128,640]{1,0:T(8,128)(2,1)} %w_ref.1, ...), custom_call_target="tpu_custom_call" | custom-call | flops 905969664 | bytes 8388608 | tf_op jit(solution)/shard_map/pallas_call | solution.py:390
  7.4 59.0 %all_to_all.10.in_v = bf16[128,112,128]{2,1,0:T(8,128)(2,1)S(1)} all-to-all(bf16[128,112,128]{2,1,0:T(8,128)(2,1)} %shard_map.118), channel_id=1, replica_groups=mesh['ch'=32,'half'=4] {'ch','half'}, dimensions={0} | all-to-all | bytes 7340032 | tf_op jit(solution)/shard_map/all_to_all | solution.py:402
  66.4 4.0 %shard_map.119 = bf16[128,72,128]{2,1,0:T(8,128)(2,1)} custom-call(bf16[128,112,128]{2,1,0:T(8,128)(2,1)S(1)} %all_to_all.10.in_v), custom_call_target="tpu_custom_call" | custom-call | flops 1811939328 | bytes 8388608 | tf_op jit(solution)/shard_map/pallas_call | solution.py:390
  70.4 5.5 %all-to-all-start.1 = ((bf16[128,72,128]{2,1,0:T(8,128)(2,1)}), bf16[128,72,128]{2,1,0:T(8,128)(2,1)}, u32[]{:S(2)}, u32[]{:S(2)}) async-start(bf16[128,72,128]{2,1,0:T(8,128)(2,1)} %shard_map.119), calls=%async_computation.1 | async-start | bytes 4718592 | tf_op jit(solution)/shard_map/all_to_all | solution.py:402
  75.9 10.7 %shard_map.120 = (bf16[12,3,6,128,128]{4,3,2,1,0:T(8,128)(2,1)}, f32[12,3,8,128]{3,2,1,0:T(8,128)}) custom-call(bf16[192,24,128]{2,1,0:T(8,128)(2,1)} %refs_0_.3, bf16[192,24,128]{2,1,0:T(8,128)(2,1)} %refs_1_.3, bf16[192,24,128]{2,1,0:T(8,128)(2,1)} %refs_2_.3, s32[768]{0:T(1024)} %refs_3_.3, s32[768]{0:T(1024)} %refs_4_.3, s32[4,4]{1,0:T(4,128)} %refs_5_.3, ...), custom_call_target="tpu_custom_call" | custom-call | flops 905969664 | bytes 12582912 | tf_op jit(solution)/shard_map/pallas_call | solution.py:390
  86.6 22.5 %all-to-all-done.1.in_ref = bf16[128,72,128]{2,1,0:T(8,128)(2,1)} async-done(((bf16[128,72,128]{2,1,0:T(8,128)(2,1)}), bf16[128,72,128]{2,1,0:T(8,128)(2,1)}, u32[]{:S(2)}, u32[]{:S(2)}) %all-to-all-start.1) | async-done | bytes 2359328 | tf_op jit(solution)/shard_map/all_to_all | solution.py:402
  109.1 5.7 %shard_map.121 = bf16[192,24,128]{2,1,0:T(8,128)(2,1)} custom-call(bf16[128,72,128]{2,1,0:T(8,128)(2,1)} %all-to-all-done.1.in_ref, bf16[12,3,6,128,128]{4,3,2,1,0:T(8,128)(2,1)} %get-tuple-element.7.saved_ref, f32[12,3,8,128]{3,2,1,0:T(8,128)} %get-tuple-element.8.inv_ref, bf16[128,640]{1,0:T(8,128)(2,1)} %w_ref.1, f32[128]{0:T(128)} %gain_ref.1), custom_call_target="tpu_custom_call" | custom-call | flops 754974720 | bytes 12582912 | tf_op jit(solution)/shard_map/pallas_call | solution.py:390
Async XLA Ops:
  70.4 38.7 %all-to-all-start.1 = ((bf16[128,72,128]{2,1,0:T(8,128)(2,1)}), bf16[128,72,128]{2,1,0:T(8,128)(2,1)}, u32[]{:S(2)}, u32[]{:S(2)}) async-start(bf16[128,72,128]{2,1,0:T(8,128)(2,1)} %shard_map.119), calls=%async_computation.1 | async-start | bytes 4718592 | tf_op jit(solution)/shard_map/all_to_all | solution.py:402

commit v7 on v6

--- a/solution.py
+++ b/solution.py
@@ -116,7 +116,8 @@
     for n in range(5):
         part = w_v[:, n * C : (n + 1) * C].astype(F32).T
         wt[n] = (part * 0.5 if n in (1, 3, 4) else part).astype(BF16)
-    for n, g in enumerate(gains[:3]):
+    wot[...] = wo_v[...].astype(F32).T.astype(BF16)
+    for n, g in enumerate(gains):
         cols[n] = column(g)
     cols[4] = cols[2] * 0.5
     find_keep(mask_v, chain_v, pairs_v, keep)
@@ -200,8 +201,6 @@
     *buffers, x, wt, wot, cols, keep, sems = refs[14:]
     tiles = buffers[-1]
     wait = prepare(given, buffers, wt, wot, cols, keep, sems)
-    wot[...] = buffers[4][...].astype(F32).T.astype(BF16)
-    cols[3] = column(buffers[8])
 
     def body(group, _):
         spread(tiles, x, group, wait)
@@ -348,22 +347,15 @@
             a, b = get(2 * GROUP + q), get(2 * GROUP + PAIRS + q)
             lefts = [get(q), get(PAIRS + q), jnp.where(low, a, swap(b))]
             rights = [get(GROUP + q), get(GROUP + PAIRS + q), jnp.where(low, swap(a), b)]
-            for parts in ((0, 1), (2,)):
-
-                def wide(take_one):
-                    return jnp.concatenate([take_one(part) for part in parts], 1)
-
-                grad_l = wide(lambda part: lefts[part].astype(BF16))
-                grad_r = wide(lambda part: rights[part].astype(BF16))
-                s0, s1, s2, s3, s4, s5 = (wide(lambda part, m=m: saved_v[n, part, m]) for m in range(6))
-                pieces = [grad_l * s0, grad_l * s1, grad_r * s2, grad_r * s3, s4]
-                e = dot(w_v[...], jnp.concatenate(pieces, 0)) * wide(lambda part: cols[...])
-                unit_z = s5.astype(F32)
-                inv = wide(lambda part: inv_v[n, part][:1])
-                grad = (inv * (e - mean(e) - unit_z * mean(e * unit_z))).T
-                if parts != (2,):
-                    put(q, grad[:C])
-                    put(q + PAIRS, grad[C:])
+            for part in range(3):
+                saved = saved_v.at[n, part]
+                grad_l, grad_r = lefts[part].astype(BF16), rights[part].astype(BF16)
+                pieces = [grad_l * saved[0], grad_l * saved[1], grad_r * saved[2], grad_r * saved[3], saved[4]]
+                e = dot(w_v[...], jnp.concatenate(pieces, 0)) * cols[...]
+                unit_z = saved[5].astype(F32)
+                grad = (inv_v[n, part][:1] * (e - mean(e) - unit_z * mean(e * unit_z))).T
+                if part < 2:
+                    put(q + PAIRS * part, grad)
                 else:
                     put(C * X_PITCH + q, grad[:64])
                     put(C * X_PITCH + PAIRS + q, grad[64:])

time: 115 us -> 115 us (level)
  no operation moved by 1% of the time
where the time goes in v7:
time: 115 us
  blocking collectives  59 us (51%)
  Pallas kernels  27.7 us (24%)
  waiting for transfers between devices  22.5 us (20%)
  starting transfers between devices  5.53 us (5%)
    all_to_all x1, blocking collectives, exchange(): return lax.all_to_all(x, AXES, split_axis=0, concat_axis=0, tiled=True)  59 us
    pallas_call x4, Pallas kernels, call(): pl.pallas_call(kernel, out_shape=outs, in_specs=ins, out_specs=out_specs,...  27.7 us
    all_to_all x1, waiting for transfers between devices, exchange(): return lax.all_to_all(x, AXES, split_axis=0, concat_axis=0, tiled=True)  22.5 us
    all_to_all x1, starting transfers between devices, exchange(): return lax.all_to_all(x, AXES, split_axis=0, concat_axis=0, tiled=True)  5.53 us
  transfers between devices with their start and end apart: 1, of which 1 were waited for; matrix products, arithmetic and copies ran while one was open for 0% of the time, Pallas kernels for 9%

profile of v7, /device:TPU:1, one launch (start us, length us, event | category | flops | bytes accessed | tf_op | source)
XLA Modules:
  0.0 114.8 jit_solution(10853855171136661293)
XLA Ops:
  0.0 7.4 %shard_map.118 = bf16[128,112,128]{2,1,0:T(8,128)(2,1)} custom-call(bf16[192,24,128]{2,1,0:T(8,128)(2,1)} %refs_0_.3, bf16[192,24,128]{2,1,0:T(8,128)(2,1)} %refs_1_.3, bf16[192,24,128]{2,1,0:T(8,128)(2,1)} %refs_2_.3, s32[768]{0:T(1024)} %refs_3_.3, s32[768]{0:T(1024)} %refs_4_.3, s32[4,4]{1,0:T(4,128)} %refs_5_.3, bf16[128,640]{1,0:T(8,128)(2,1)} %w_ref.1, ...), custom_call_target="tpu_custom_call" | custom-call | flops 905969664 | bytes 8388608 | tf_op jit(solution)/shard_map/pallas_call | solution.py:382
  7.4 59.0 %all_to_all.10.in_v = bf16[128,112,128]{2,1,0:T(8,128)(2,1)S(1)} all-to-all(bf16[128,112,128]{2,1,0:T(8,128)(2,1)} %shard_map.118), channel_id=1, replica_groups=mesh['ch'=32,'half'=4] {'ch','half'}, dimensions={0} | all-to-all | bytes 7340032 | tf_op jit(solution)/shard_map/all_to_all | solution.py:394
  66.4 4.0 %shard_map.119 = bf16[128,72,128]{2,1,0:T(8,128)(2,1)} custom-call(bf16[128,112,128]{2,1,0:T(8,128)(2,1)S(1)} %all_to_all.10.in_v), custom_call_target="tpu_custom_call" | custom-call | flops 1811939328 | bytes 8388608 | tf_op jit(solution)/shard_map/pallas_call | solution.py:382
  70.4 5.5 %all-to-all-start.1 = ((bf16[128,72,128]{2,1,0:T(8,128)(2,1)}), bf16[128,72,128]{2,1,0:T(8,128)(2,1)}, u32[]{:S(2)}, u32[]{:S(2)}) async-start(bf16[128,72,128]{2,1,0:T(8,128)(2,1)} %shard_map.119), calls=%async_computation.1 | async-start | bytes 4718592 | tf_op jit(solution)/shard_map/all_to_all | solution.py:394
  75.9 10.7 %shard_map.120 = (bf16[12,3,6,128,128]{4,3,2,1,0:T(8,128)(2,1)}, f32[12,3,8,128]{3,2,1,0:T(8,128)}) custom-call(bf16[192,24,128]{2,1,0:T(8,128)(2,1)} %refs_0_.3, bf16[192,24,128]{2,1,0:T(8,128)(2,1)} %refs_1_.3, bf16[192,24,128]{2,1,0:T(8,128)(2,1)} %refs_2_.3, s32[768]{0:T(1024)} %refs_3_.3, s32[768]{0:T(1024)} %refs_4_.3, s32[4,4]{1,0:T(4,128)} %refs_5_.3, ...), custom_call_target="tpu_custom_call" | custom-call | flops 905969664 | bytes 12582912 | tf_op jit(solution)/shard_map/pallas_call | solution.py:382
  86.6 22.5 %all-to-all-done.1.in_ref = bf16[128,72,128]{2,1,0:T(8,128)(2,1)} async-done(((bf16[128,72,128]{2,1,0:T(8,128)(2,1)}), bf16[128,72,128]{2,1,0:T(8,128)(2,1)}, u32[]{:S(2)}, u32[]{:S(2)}) %all-to-all-start.1) | async-done | bytes 2359328 | tf_op jit(solution)/shard_map/all_to_all | solution.py:394
  109.1 5.7 %shard_map.121 = bf16[192,24,128]{2,1,0:T(8,128)(2,1)} custom-call(bf16[128,72,128]{2,1,0:T(8,128)(2,1)} %all-to-all-done.1.in_ref, bf16[12,3,6,128,128]{4,3,2,1,0:T(8,128)(2,1)} %get-tuple-element.7.saved_ref, f32[12,3,8,128]{3,2,1,0:T(8,128)} %get-tuple-element.8.inv_ref, bf16[128,640]{1,0:T(8,128)(2,1)} %w_ref.1, f32[128]{0:T(128)} %gain_ref.1), custom_call_target="tpu_custom_call" | custom-call | flops 754974720 | bytes 12582912 | tf_op jit(solution)/shard_map/pallas_call | solution.py:382
Async XLA Ops:
  70.4 38.7 %all-to-all-start.1 = ((bf16[128,72,128]{2,1,0:T(8,128)(2,1)}), bf16[128,72,128]{2,1,0:T(8,128)(2,1)}, u32[]{:S(2)}, u32[]{:S(2)}) async-start(bf16[128,72,128]{2,1,0:T(8,128)(2,1)} %shard_map.119), calls=%async_computation.1 | async-start | bytes 4718592 | tf_op jit(solution)/shard_map/all_to_all | solution.py:394
